TPU v7x, 256 devices: a whole 4x4x8 slice. The times are simulated.
256 devices in a mesh: grp: 8 (over z), dev: 32 (over x, y, core).
Axes of the slice: x: 4, y: 4, z: 8, core: 2. Of those that a mesh axis runs over, the one named last changes fastest.
Arguments:
- matrix: float32 [524288, 1024], P(('grp', 'dev')), may hold values from -60 to 60
- block_order: int32 [8, 512], P('grp'), may hold values from 0 to 511, as said below
- counts: int32 [8, 32], P('grp'), may hold values from 0 to 32, as said below
- sign_bits: int32 [8, 512, 128], P('grp'), may hold values from 0 to 1
- row_mask: int32 [8, 512, 128], P('grp'), may hold values from 0 to 1, as said below
Outputs:
- sketch: float32 [262144, 1024], P(('grp', 'dev'))
- group_factor: float32 [8, 1024, 1024], P('grp', 'dev')
- factor: float32 [1024, 1024], P('dev')
Inputs may be any that keep to these rules, and one draw needn't show every extreme that they name: Each row of block_order is a permutation of the group's block indices; at most 1 block of one device's blocks are placed in the positions held by one device, and some pair reaches 1. `counts`: each row sums to 512; its largest entry is exactly 32. `row_mask`: exactly 32 ones in each row of 128.
All inputs are finite; a program needn't handle non-finite values.
Results may differ from a plain program's by a relative error of at most 0.0003.
Values sent between devices are 32-bit elements; how exact they have to be, the bound alone decides.
A program may use at most 128 MiB of HBM per device.

v0:
```python
import jax
import jax.numpy as jnp
from jax import lax
from jax.sharding import PartitionSpec as P

BLOCK = 128
KEEP = 32


def hadamard(order_of):
    indices = jnp.arange(order_of, dtype=jnp.int32)
    common = jnp.bitwise_and(indices[:, None], indices[None, :])
    parity = jnp.zeros_like(common)
    for shift_by in range(order_of.bit_length() - 1):
        parity = parity + jnp.bitwise_and(jnp.right_shift(common, shift_by), 1)
    return (1 - 2 * (parity % 2)).astype(jnp.float32)


def mix_blocks(block_list, mask_rows, sign_rows, walsh_sign_matrix):
    running = jnp.cumsum(mask_rows, axis=1) - 1
    choose_row = jnp.arange(KEEP, dtype=jnp.int32)[None, :, None]
    select_rows = ((mask_rows[:, None, :] == 1) & (running[:, None, :] == choose_row)).astype(
        jnp.float32
    )
    mixing_transform = jnp.einsum(
        "jlf,fp->jlp", select_rows, walsh_sign_matrix, precision=lax.Precision.HIGHEST
    )
    mixing_transform = mixing_transform * (1 - 2 * sign_rows).astype(jnp.float32)[:, None, :]
    normalize_rows = float(walsh_sign_matrix.shape[0]) ** (-0.5)
    return (
        jnp.einsum("uwd,udk->uwk", mixing_transform, block_list, precision=lax.Precision.HIGHEST)
        * normalize_rows
    )


def gram_of(mixed_rows):
    flat_rows = mixed_rows.reshape(-1, mixed_rows.shape[-1])
    return jnp.einsum("kc,ke->ce", flat_rows, flat_rows, precision=lax.Precision.HIGHEST)


def body(matrix, block_order, counts, sign_bits, row_mask):
    blocks_dev = matrix.shape[0] // BLOCK
    columns = matrix.shape[1]
    devices = lax.axis_size("dev")
    groups = lax.axis_size("grp")
    me_dev = lax.axis_index("dev")
    positions = devices * blocks_dev
    most_held = 2 * blocks_dev
    capacity = max(1, 2 * blocks_dev // devices)
    order_row = block_order[0]
    count_row = counts[0]
    sign_table = sign_bits[0]
    mask_table = row_mask[0]
    run_ends = jnp.cumsum(count_row)
    offsets = run_ends - count_row
    block_locations = jnp.arange(positions, dtype=jnp.int32)
    owners = jnp.sum((block_locations[:, None] >= run_ends[None, :]).astype(jnp.int32), axis=1)
    source = order_row // blocks_dev
    earlier = (
        (block_locations[None, :] < block_locations[:, None])
        & (owners[None, :] == owners[:, None])
        & (source[None, :] == source[:, None])
    )
    slot_of = jnp.sum(earlier.astype(jnp.int32), axis=1)
    target = owners * capacity + slot_of
    inverse = jnp.zeros((positions,), jnp.int32).at[order_row].set(block_locations)
    my_places = lax.dynamic_slice_in_dim(inverse, me_dev * blocks_dev, blocks_dev)
    my_target = target[my_places]
    buffer_slots = jnp.arange(devices * capacity, dtype=jnp.int32)
    matches = my_target[None, :] == buffer_slots[:, None]
    filled = jnp.any(matches, axis=1)
    pick_block = jnp.sum(
        matches.astype(jnp.int32) * jnp.arange(blocks_dev, dtype=jnp.int32)[None, :], axis=1
    )
    held_slots = jnp.arange(most_held, dtype=jnp.int32)
    my_count = lax.dynamic_index_in_dim(count_row, me_dev, 0, False)
    my_offset = lax.dynamic_index_in_dim(offsets, me_dev, 0, False)
    live_slot = held_slots < my_count
    my_positions = jnp.minimum(my_offset + held_slots, positions - 1)
    from_slot = source[my_positions] * capacity + slot_of[my_positions]
    local_blocks = matrix.reshape(blocks_dev, BLOCK, columns)
    walsh_sign_matrix = hadamard(BLOCK)
    outgoing = jnp.where(filled[:, None, None], jnp.take(local_blocks, pick_block, axis=0), 0.0)
    arrived = lax.all_to_all(outgoing, "dev", split_axis=0, concat_axis=0, tiled=True)
    my_blocks = jnp.take(arrived, from_slot, axis=0)
    mixed_rows = mix_blocks(
        my_blocks, mask_table[my_positions], sign_table[my_positions], walsh_sign_matrix
    )
    sketch = jnp.where(live_slot[:, None, None], mixed_rows, 0.0)
    partial_value = gram_of(sketch)
    group_gram = lax.psum(partial_value, "dev") / float(positions * KEEP)
    mean_gram = lax.psum(group_gram, "grp") / float(groups)
    rows_dev = columns // devices
    group_upper = jnp.linalg.cholesky(group_gram).T
    mean_upper = jnp.linalg.cholesky(mean_gram).T
    group_factor = lax.dynamic_slice_in_dim(group_upper, me_dev * rows_dev, rows_dev, 0)[None]
    factor = lax.dynamic_slice_in_dim(mean_upper, me_dev * rows_dev, rows_dev, 0)
    return (sketch.reshape(most_held * KEEP, columns), group_factor, factor)


def solution(mesh):
    placed = (
        P(("grp", "dev"), None),
        P("grp", None),
        P("grp", None),
        P("grp", None, None),
        P("grp", None, None),
    )
    return jax.shard_map(
        body,
        mesh=mesh,
        in_specs=placed,
        out_specs=(P(("grp", "dev"), None), P("grp", "dev", None), P("dev", None)),
        check_vma=False,
    )
```

profile of v0, /device:TPU:1, one launch (start us, length us, event | category | flops | bytes accessed | tf_op | source)
XLA Modules:
  0.0 938.6 jit_solution(11995743199234559073)
XLA Ops:
  10.3 2.4 scatter_custom_fusion
  16.0 11.5 %gather_fusion.5 = f32[32,128,1024]{2,1,0:T(8,128)} fusion(f32[16,128,1024]{2,1,0:T(8,128)} %bitcast.119, s32[1024]{0:T(1024)S(1)} %pad_clamp_fusion.1), kind=kCustom, calls=%fused_computation.5 | custom fusion | bytes 33554560 | tf_op jit(solution)/shard_map/jit(_take)/gather | solution.py:83
  27.5 12.6 %select_select_fusion = f32[32,128,1024]{2,1,0:T(8,128)} fusion(f32[32,128,1024]{2,1,0:T(8,128)} %gather_fusion.5, pred[32]{0:T(512)(128)(4,1)S(1)} %compare_and_fusion, pred[32]{0:T(512)(128)(4,1)S(1)} %fusion.88), kind=kLoop, calls=%fused_computation.10 | loop fusion | flops 8388608 | bytes 33554496 | tf_op jit(solution)/shard_map/jit(_where)/select_n | solution.py:83
  40.1 8.8 all-to-all-start
  53.7 226.5 %all-to-all-done = f32[32,128,1024]{2,1,0:T(8,128)} async-done(((f32[32,128,1024]{2,1,0:T(8,128)}), f32[32,128,1024]{2,1,0:T(8,128)}, u32[]{:S(2)}, u32[]{:S(2)}) %all-to-all-start) | async-done | bytes 16777248 | tf_op jit(solution)/shard_map/all_to_all | solution.py:84
  280.1 14.3 %gather_fusion.6 = f32[32,128,1024]{2,1,0:T(8,128)} fusion(f32[32,128,1024]{2,1,0:T(8,128)} %all-to-all-done, s32[1024]{0:T(1024)S(1)} %pad_clamp_fusion), kind=kCustom, calls=%fused_computation.6 | custom fusion | bytes 33554560 | tf_op jit(solution)/shard_map/jit(_take)/gather | solution.py:85
  294.4 12.2 %multiply_select_fusion = f32[32,32,1024]{2,1,0:T(8,128)S(1)} fusion(pred[32]{0:T(512)(128)(4,1)S(1)} %iota_compare_fusion.7, f32[32,32,128]{2,1,0:T(8,128)S(1)} %convolution_multiply_fusion, f32[32,128,1024]{2,1,0:T(8,128)} %gather_fusion.6, pred[32]{0:T(512)(128)(4,1)S(1)} %compare_and_fusion.1), kind=kOutput, calls=%fused_computation.18 | convolution fusion | flops 1616904192 | bytes 21495872 | tf_op jit(solution)/shard_map/uwd,udk->uwk/dot_general | solution.py:31
  308.6 14.9 %convolution_bitcast_fusion = f32[1024,1024]{0,1:T(8,128)} fusion(f32[32,32,1024]{2,1,0:T(8,128)S(1)} %multiply_select_fusion), kind=kOutput, calls=%fused_computation.19 | convolution fusion | flops 12884901888 | bytes 8388608 | tf_op jit(solution)/shard_map/kc,ke->ce/dot_general | solution.py:38
  323.8 161.1 %all-reduce.4.cloned.1.call-done = f32[1024,1024]{0,1:T(8,128)} async-done(((f32[1024,1024]{0,1:T(8,128)}), f32[1024,1024]{0,1:T(8,128)}) %all-reduce.4.cloned.1.call-update) | async-done | bytes 4194320 | tf_op jit(solution)/shard_map/psum | solution.py:91
  484.9 5.0 broadcast_multiply_fusion.1
  489.9 5.3 copy.50
  495.6 4.4 fusion.5
  502.0 11.7 %cholesky.619 = f32[128,128]{1,0:T(8,128)S(1)} custom-call(f32[128,128]{1,0:T(8,128)S(1)} %cholesky.911), custom_call_target="Cholesky" | custom-call | tf_op jit(solution)/shard_map/jit(cholesky)/cholesky | solution.py:94
  513.8 9.8 %custom-call.51 = f32[1,128,128]{1,2,0:T(8,128)S(1)} custom-call(f32[1,128,128]{2,1,0:T(8,128)S(1)} %get-tuple-element.58), custom_call_target="InvertDiagBlocksLowerTriangular" | custom-call | tf_op jit(solution)/shard_map/jit(cholesky)/cholesky | solution.py:94
  527.4 2.5 cholesky.645
  529.9 11.9 %cholesky.638 = f32[128,128]{1,0:T(8,128)S(1)} custom-call(f32[128,128]{1,0:T(8,128)S(1)} %cholesky.915), custom_call_target="Cholesky" | custom-call | tf_op jit(solution)/shard_map/jit(cholesky)/cholesky | solution.py:94
  543.3 9.8 %custom-call.52 = f32[1,128,128]{1,2,0:T(8,128)S(1)} custom-call(f32[1,128,128]{2,1,0:T(8,128)S(1)} %get-tuple-element.55), custom_call_target="InvertDiagBlocksLowerTriangular" | custom-call | tf_op jit(solution)/shard_map/jit(cholesky)/cholesky | solution.py:94
  556.5 11.7 %cholesky.659 = f32[128,128]{1,0:T(8,128)S(1)} custom-call(f32[128,128]{1,0:T(8,128)S(1)} %cholesky.920), custom_call_target="Cholesky" | custom-call | tf_op jit(solution)/shard_map/jit(cholesky)/cholesky | solution.py:94
  568.8 9.8 %custom-call.53 = f32[1,128,128]{1,2,0:T(8,128)S(1)} custom-call(f32[1,128,128]{2,1,0:T(8,128)S(1)} %get-tuple-element.52), custom_call_target="InvertDiagBlocksLowerTriangular" | custom-call | tf_op jit(solution)/shard_map/jit(cholesky)/cholesky | solution.py:94
  579.8 2.4 convolution_subtract_fusion.5
  582.2 11.9 %cholesky.678 = f32[128,128]{1,0:T(8,128)S(1)} custom-call(f32[128,128]{1,0:T(8,128)S(1)} %cholesky.925), custom_call_target="Cholesky" | custom-call | tf_op jit(solution)/shard_map/jit(cholesky)/cholesky | solution.py:94
  594.8 9.8 %custom-call.54 = f32[1,128,128]{1,2,0:T(8,128)S(1)} custom-call(f32[1,128,128]{2,1,0:T(8,128)S(1)} %get-tuple-element.49), custom_call_target="InvertDiagBlocksLowerTriangular" | custom-call | tf_op jit(solution)/shard_map/jit(cholesky)/cholesky | solution.py:94
  608.1 11.7 %cholesky.697 = f32[128,128]{1,0:T(8,128)S(1)} custom-call(f32[128,128]{1,0:T(8,128)S(1)} %cholesky.930), custom_call_target="Cholesky" | custom-call | tf_op jit(solution)/shard_map/jit(cholesky)/cholesky | solution.py:94
  620.4 10.2 %custom-call.55 = f32[1,128,128]{1,2,0:T(8,128)S(1)} custom-call(f32[1,128,128]{2,1,0:T(8,128)S(1)} %get-tuple-element.46), custom_call_target="InvertDiagBlocksLowerTriangular" | custom-call | tf_op jit(solution)/shard_map/jit(cholesky)/cholesky | solution.py:94
  634.0 11.7 %cholesky.716 = f32[128,128]{1,0:T(8,128)S(1)} custom-call(f32[128,128]{1,0:T(8,128)S(1)} %cholesky.935), custom_call_target="Cholesky" | custom-call | tf_op jit(solution)/shard_map/jit(cholesky)/cholesky | solution.py:94
  646.3 9.8 %custom-call.56 = f32[1,128,128]{1,2,0:T(8,128)S(1)} custom-call(f32[1,128,128]{2,1,0:T(8,128)S(1)} %get-tuple-element.43), custom_call_target="InvertDiagBlocksLowerTriangular" | custom-call | tf_op jit(solution)/shard_map/jit(cholesky)/cholesky | solution.py:94
  659.1 11.9 %cholesky.735 = f32[128,128]{1,0:T(8,128)S(1)} custom-call(f32[128,128]{1,0:T(8,128)S(1)} %cholesky.940), custom_call_target="Cholesky" | custom-call | tf_op jit(solution)/shard_map/jit(cholesky)/cholesky | solution.py:94
  671.6 9.8 %custom-call.57 = f32[1,128,128]{1,2,0:T(8,128)S(1)} custom-call(f32[1,128,128]{2,1,0:T(8,128)S(1)} %get-tuple-element.40), custom_call_target="InvertDiagBlocksLowerTriangular" | custom-call | tf_op jit(solution)/shard_map/jit(cholesky)/cholesky | solution.py:94
  684.1 11.7 %cholesky.752 = f32[128,128]{1,0:T(8,128)S(1)} custom-call(f32[128,128]{1,0:T(8,128)S(1)} %convolution_subtract_fusion.13), custom_call_target="Cholesky" | custom-call | tf_op jit(solution)/shard_map/jit(cholesky)/cholesky | solution.py:94
  706.7 5.0 broadcast_multiply_fusion
  711.7 5.5 copy.58
  717.3 4.4 fusion.4
  723.7 11.7 %cholesky.767 = f32[128,128]{1,0:T(8,128)S(1)} custom-call(f32[128,128]{1,0:T(8,128)S(1)} %cholesky.947), custom_call_target="Cholesky" | custom-call | tf_op jit(solution)/shard_map/jit(cholesky)/cholesky | solution.py:95
  735.4 2.5 cholesky.793
  737.9 9.8 %custom-call.58 = f32[1,128,128]{1,2,0:T(8,128)S(1)} custom-call(f32[1,128,128]{2,1,0:T(8,128)S(1)} %get-tuple-element.36), custom_call_target="InvertDiagBlocksLowerTriangular" | custom-call | tf_op jit(solution)/shard_map/jit(cholesky)/cholesky | solution.py:95
  751.5 12.1 %cholesky.786 = f32[128,128]{1,0:T(8,128)S(1)} custom-call(f32[128,128]{1,0:T(8,128)S(1)} %cholesky.951), custom_call_target="Cholesky" | custom-call | tf_op jit(solution)/shard_map/jit(cholesky)/cholesky | solution.py:95
  766.4 9.8 %custom-call.59 = f32[1,128,128]{1,2,0:T(8,128)S(1)} custom-call(f32[1,128,128]{2,1,0:T(8,128)S(1)} %get-tuple-element.33), custom_call_target="InvertDiagBlocksLowerTriangular" | custom-call | tf_op jit(solution)/shard_map/jit(cholesky)/cholesky | solution.py:95
  779.6 11.7 %cholesky.807 = f32[128,128]{1,0:T(8,128)S(1)} custom-call(f32[128,128]{1,0:T(8,128)S(1)} %cholesky.956), custom_call_target="Cholesky" | custom-call | tf_op jit(solution)/shard_map/jit(cholesky)/cholesky | solution.py:95
  792.5 9.8 %custom-call.60 = f32[1,128,128]{1,2,0:T(8,128)S(1)} custom-call(f32[1,128,128]{2,1,0:T(8,128)S(1)} %get-tuple-element.30), custom_call_target="InvertDiagBlocksLowerTriangular" | custom-call | tf_op jit(solution)/shard_map/jit(cholesky)/cholesky | solution.py:95
  805.8 11.9 %cholesky.826 = f32[128,128]{1,0:T(8,128)S(1)} custom-call(f32[128,128]{1,0:T(8,128)S(1)} %cholesky.961), custom_call_target="Cholesky" | custom-call | tf_op jit(solution)/shard_map/jit(cholesky)/cholesky | solution.py:95
  819.0 9.8 %custom-call.61 = f32[1,128,128]{1,2,0:T(8,128)S(1)} custom-call(f32[1,128,128]{2,1,0:T(8,128)S(1)} %get-tuple-element.27), custom_call_target="InvertDiagBlocksLowerTriangular" | custom-call | tf_op jit(solution)/shard_map/jit(cholesky)/cholesky | solution.py:95
  832.3 11.7 %cholesky.845 = f32[128,128]{1,0:T(8,128)S(1)} custom-call(f32[128,128]{1,0:T(8,128)S(1)} %cholesky.966), custom_call_target="Cholesky" | custom-call | tf_op jit(solution)/shard_map/jit(cholesky)/cholesky | solution.py:95
  845.3 10.0 %custom-call.62 = f32[1,128,128]{1,2,0:T(8,128)S(1)} custom-call(f32[1,128,128]{2,1,0:T(8,128)S(1)} %get-tuple-element.24), custom_call_target="InvertDiagBlocksLowerTriangular" | custom-call | tf_op jit(solution)/shard_map/jit(cholesky)/cholesky | solution.py:95
  858.6 11.7 %cholesky.864 = f32[128,128]{1,0:T(8,128)S(1)} custom-call(f32[128,128]{1,0:T(8,128)S(1)} %cholesky.971), custom_call_target="Cholesky" | custom-call | tf_op jit(solution)/shard_map/jit(cholesky)/cholesky | solution.py:95
  871.6 9.8 %custom-call.63 = f32[1,128,128]{1,2,0:T(8,128)S(1)} custom-call(f32[1,128,128]{2,1,0:T(8,128)S(1)} %get-tuple-element.21), custom_call_target="InvertDiagBlocksLowerTriangular" | custom-call | tf_op jit(solution)/shard_map/jit(cholesky)/cholesky | solution.py:95
  884.4 11.9 %cholesky.883 = f32[128,128]{1,0:T(8,128)S(1)} custom-call(f32[128,128]{1,0:T(8,128)S(1)} %cholesky.976), custom_call_target="Cholesky" | custom-call | tf_op jit(solution)/shard_map/jit(cholesky)/cholesky | solution.py:95
  897.6 9.8 %custom-call.64 = f32[1,128,128]{1,2,0:T(8,128)S(1)} custom-call(f32[1,128,128]{2,1,0:T(8,128)S(1)} %get-tuple-element.18), custom_call_target="InvertDiagBlocksLowerTriangular" | custom-call | tf_op jit(solution)/shard_map/jit(cholesky)/cholesky | solution.py:95
  910.0 11.7 %cholesky.900 = f32[128,128]{1,0:T(8,128)S(1)} custom-call(f32[128,128]{1,0:T(8,128)S(1)} %convolution_subtract_fusion.12), custom_call_target="Cholesky" | custom-call | tf_op jit(solution)/shard_map/jit(cholesky)/cholesky | solution.py:95
  (135 shorter events, 85.7 us)
Async XLA Ops:
  7.2 43.8 %copy-start = (s32[1,512,128]{2,1,0:T(8,128)S(1)}, s32[1,512,128]{2,1,0:T(8,128)}, u32[]{:S(2)}) copy-start(s32[1,512,128]{2,1,0:T(8,128)} %param.10) | copy-start | bytes 786436
  40.1 10.4 %copy-start.6 = (s32[1,32]{1,0:T(1,128)S(1)}, s32[1,32]{1,0:T(1,128)}, u32[]{:S(2)}) copy-start(s32[1,32]{1,0:T(1,128)} %param.8) | copy-start | bytes 388
  40.1 11.8 %copy-start.5 = (s32[1,512,128]{2,1,0:T(8,128)S(1)}, s32[1,512,128]{2,1,0:T(8,128)}, u32[]{:S(2)}) copy-start(s32[1,512,128]{2,1,0:T(8,128)} %param.9) | copy-start | bytes 786436
  40.1 240.0 %all-to-all-start = ((f32[32,128,1024]{2,1,0:T(8,128)}), f32[32,128,1024]{2,1,0:T(8,128)}, u32[]{:S(2)}, u32[]{:S(2)}) async-start(f32[32,128,1024]{2,1,0:T(8,128)} %select_select_fusion), calls=%async_computation | async-start | bytes 33554432 | tf_op jit(solution)/shard_map/all_to_all | solution.py:84
  48.9 436.0 %all-reduce.4.cloned.1.call-start = ((), (), s32[]{:S(2)}) async-start(), calls=%async_computation.1 | async-start | bytes 8388608 | tf_op jit(solution)/shard_map/psum | solution.py:91
  306.6 2.0 copy-start.2
  495.2 211.5 %all-reduce.6.cloned.1.call-start = ((), (), s32[]{:S(2)}) async-start(), calls=%async_computation.2 | async-start | bytes 8388608 | tf_op jit(solution)/shard_map/psum | solution.py:92
  500.1 2.0 copy-start.4
  721.7 1.9 copy-start.3
  855.3 76.1 %copy-start.1 = (s32[1,512,128]{2,1,0:T(8,128)S(1)}, s32[1,512,128]{2,1,0:T(8,128)}, u32[]{:S(2)}) copy-start(s32[1,512,128]{2,1,0:T(8,128)} %param.10) | copy-start | bytes 786436
Sparse Core Ops, SparseCore 0:
  323.6 161.2 all-reduce.3
  527.5 108.8 all-reduce.5
where the time goes:
time: 944 us; the launch traced here: 939 us
  waiting for transfers between devices  388 us (41%)
  other arithmetic  385 us (41%)
  matrix products  73 us (8%)
  local copies, waits for them, and re-layouts  59.1 us (6%)
  between operations  25.2 us (3%)
    all_to_all x1, waiting for transfers between devices, body(): lax.all_to_all(outgoing, 'dev', split_axis=0, concat_axis=0, tiled=True)  226 us
    another operation x31, other arithmetic, body(): mean_upper = jnp.linalg.cholesky(mean_gram).T  173 us
    another operation x31, other arithmetic, body(): group_upper = jnp.linalg.cholesky(group_gram).T  173 us
    psum x1, waiting for transfers between devices, body(): group_gram = lax.psum(partial_value, 'dev') / float(positions * KEEP)  161 us
    another operation x14, matrix products, body(): group_upper = jnp.linalg.cholesky(group_gram).T  22.8 us
    another operation x14, matrix products, body(): mean_upper = jnp.linalg.cholesky(mean_gram).T  22.7 us
  transfers between devices with their start and end apart: 3, of which 2 were waited for; matrix products, arithmetic and copies ran while one was open for 19% of the time, Pallas kernels for 0%

commit v1 on v0

v1 whole, which is shorter than its diff:
```python
import jax
import jax.numpy as jnp
from jax import lax
from jax.experimental import pallas as pl
from jax.experimental.pallas import tpu as pltpu
from jax.sharding import PartitionSpec as P

MESH = pl.DeviceIdType.MESH
F32, BF16, I32 = jnp.float32, jnp.bfloat16, jnp.int32
BLOCK = 128
KEEP = 32
NB = 128
COLS = 1024
NBLK = COLS // NB
PER = 16
POSITIONS = 512
DEVS = 32
GRPS = 8
CHIPS = 16
SHARD = NBLK * (NBLK + 1) // 2 * NB // DEVS
ZROWS = 24


def packed(i, j):
    return i * NBLK - i * (i - 1) // 2 + (j - i)


def split2(x):
    h = x.astype(BF16)
    return h, (x - h.astype(F32)).astype(BF16)


def dot_t(a, b):
    return lax.dot_general(a, b, (((0,), (0,)), ((), ())), preferred_element_type=F32)


def dot_n(a, b):
    return lax.dot_general(a, b, (((1,), (0,)), ((), ())), preferred_element_type=F32)


def mix_kernel(order_in, counts_in, matrix, sign_bits, row_mask, send, gram, x, order, counts, signs, masks, s_rows, s_hi, s_mid, gram_v, place, tab_sem, in_sem, out_sem, gram_sem):
    me = lax.axis_index("dev")

    def fetch(k):
        return pltpu.make_async_copy(
            matrix.at[pl.ds(k * BLOCK, BLOCK)], x.at[pl.ds(k * BLOCK, BLOCK)], in_sem.at[k]
        )

    pairs = ((order_in, order), (counts_in, counts), (sign_bits, signs), (row_mask, masks))
    tables = [pltpu.make_async_copy(a, b, tab_sem.at[i]) for i, (a, b) in enumerate(pairs)]
    for table in tables:
        table.start()
    for k in range(PER):
        fetch(k).start()
    tables[0].wait()
    tables[1].wait()

    def find(p, carry):
        b = order[0, p]
        place[jnp.where((b >> 4) == me, b & 15, PER)] = p
        return carry

    lax.fori_loop(0, POSITIONS, find, 0, unroll=8)
    pos = [place[k] for k in range(PER)]

    def count(e, carry):
        run, owners = carry
        run = run + counts[0, e]
        return run, tuple(o + (p >= run).astype(I32) for o, p in zip(owners, pos))

    _, owners = lax.fori_loop(0, DEVS, count, (jnp.int32(0), (jnp.int32(0),) * PER))

    row = lax.broadcasted_iota(I32, (BLOCK, BLOCK), 0)
    col = lax.broadcasted_iota(I32, (BLOCK, BLOCK), 1)
    parity = row & col
    for shift in (4, 2, 1):
        parity = parity ^ (parity >> shift)
    walsh = (1 - 2 * (parity & 1)).astype(F32).astype(BF16)
    upto = jnp.where(row <= col, 1.0, 0.0).astype(BF16)
    tables[2].wait()
    tables[3].wait()
    mask = jnp.concatenate([masks[0, pl.ds(p, 1), :] for p in pos], axis=0).astype(F32)
    sign = jnp.concatenate([signs[0, pl.ds(p, 1), :] for p in pos], axis=0)
    sign = (1 - 2 * sign).astype(F32)
    running = dot_n(mask.astype(BF16), upto).astype(I32)
    nth = lax.broadcasted_iota(I32, (KEEP, BLOCK), 0) + 1
    chosen = [
        jnp.where((running[k : k + 1] == nth) & (mask[k : k + 1] > 0.5), 1.0, 0.0) for k in range(PER)
    ]
    mixing = dot_n(jnp.concatenate(chosen, axis=0).astype(BF16), walsh)

    outs = []
    for k in range(PER):
        t = (mixing[k * KEEP : (k + 1) * KEEP] * sign[k : k + 1]).astype(BF16)
        fetch(k).wait()
        block = x[k * BLOCK : (k + 1) * BLOCK, :]
        hi = block.astype(BF16)
        rest = block - hi.astype(F32)
        mid = rest.astype(BF16)
        low = (rest - mid.astype(F32)).astype(BF16)
        mixed = dot_n(t, hi) + dot_n(t, mid) + dot_n(t, low)
        mixed = mixed * float(BLOCK) ** -0.5
        rows = slice(k * KEEP, (k + 1) * KEEP)
        s_rows[rows, :] = mixed
        hi, mid = split2(mixed)
        s_hi[rows, :] = hi
        s_mid[rows, :] = mid
        out = pltpu.make_async_copy(s_rows.at[rows], send.at[owners[k]], out_sem.at[k])
        out.start()
        outs.append(out)

    for i in range(NBLK):
        a, b = i * NB, (i + 1) * NB
        block = dot_t(s_hi[:, a:b], s_hi[:, a:]) + dot_t(s_hi[:, a:b], s_mid[:, a:])
        block = block + dot_t(s_mid[:, a:b], s_hi[:, a:])
        for j in range(i, NBLK):
            at = packed(i, j) * NB
            gram_v[at : at + NB, :] = block[:, (j - i) * NB : (j - i + 1) * NB]
        rows = pl.ds(packed(i, i) * NB, (NBLK - i) * NB)
        out = pltpu.make_async_copy(gram_v.at[rows], gram.at[rows], gram_sem.at[i])
        out.start()
        outs.append(out)
    for out in outs:
        out.wait()


def mix(matrix, block_order, counts, sign_bits, row_mask):
    hbm = pl.BlockSpec(memory_space=pltpu.HBM)
    rows = PER * KEEP
    return pl.pallas_call(
        mix_kernel,
        out_shape=(
            jax.ShapeDtypeStruct((DEVS, KEEP, COLS), F32),
            jax.ShapeDtypeStruct((DEVS * SHARD, NB), F32),
        ),
        in_specs=[hbm] * 5,
        out_specs=(hbm, hbm),
        scratch_shapes=[
            pltpu.VMEM((PER * BLOCK, COLS), F32),
            pltpu.SMEM((1, POSITIONS), I32),
            pltpu.SMEM((1, DEVS), I32),
            pltpu.VMEM((1, POSITIONS, BLOCK), I32),
            pltpu.VMEM((1, POSITIONS, BLOCK), I32),
            pltpu.VMEM((rows, COLS), F32),
            pltpu.VMEM((rows, COLS), BF16),
            pltpu.VMEM((rows, COLS), BF16),
            pltpu.VMEM((DEVS * SHARD, NB), F32),
            pltpu.SMEM((PER + 1,), I32),
            pltpu.SemaphoreType.DMA((4,)),
            pltpu.SemaphoreType.DMA((PER,)),
            pltpu.SemaphoreType.DMA((PER,)),
            pltpu.SemaphoreType.DMA((NBLK,)),
        ],
        compiler_params=pltpu.CompilerParams(vmem_limit_bytes=62 << 20),
        name="mix_rows",
    )(block_order, counts, matrix, sign_bits, row_mask)


def reduce_kernel(g, full, mine, pair_buf, chip_buf, own, z_buf, z_sum, z_all, mean, own_sem, pair_sem, chip_sem, z_sem, m_sem, all_sem):
    grp = lax.axis_index("grp")
    dev = lax.axis_index("dev")
    core = lax.rem(dev, 2)
    chip = dev // 2
    cx, cy = chip // 4, lax.rem(chip, 4)

    def chip_at(d):
        return lax.rem(cx + d // 4, 4) * 4 + lax.rem(cy + lax.rem(d, 4), 4)

    def chip_back(d):
        return lax.rem(cx + 4 - d // 4, 4) * 4 + lax.rem(cy + 4 - lax.rem(d, 4), 4)

    def copy(src, dst, sem, at, to_grp, to_dev):
        return pltpu.make_async_remote_copy(
            src_ref=src,
            dst_ref=dst,
            send_sem=sem.at[(0, *at)],
            recv_sem=sem.at[(1, *at)],
            device_id=(to_grp, to_dev),
            device_id_type=MESH,
        )

    def z_start(z):
        return pl.multiple_of((z * 15) // 7 * 8, 8)

    partner = chip * 2 + 1 - core
    keep = pltpu.make_async_copy(g.at[core], mine, own_sem)
    keep.start()
    barrier = pltpu.get_barrier_semaphore()

    def greet(to_grp, to_dev):
        pl.semaphore_signal(barrier, inc=1, device_id=(to_grp, to_dev), device_id_type=MESH)

    greet(grp, partner)

    def greet_chip(d, c):
        greet(grp, chip_at(d) * 2)
        greet(grp, chip_at(d) * 2 + 1)
        return c

    def greet_z(d, c):
        greet(lax.rem(grp + d, GRPS), dev)
        return c

    lax.fori_loop(1, CHIPS, greet_chip, 0)
    lax.fori_loop(1, GRPS, greet_z, 0)
    pl.semaphore_wait(barrier, 1 + 2 * (CHIPS - 1) + GRPS - 1)

    pair = copy(g.at[1 - core], pair_buf, pair_sem, (), grp, partner)
    pair.start()
    keep.wait()
    pair.wait()

    def add_pair(i, c):
        pair_buf[i] = pair_buf[i] + mine[i]
        return c

    lax.fori_loop(0, CHIPS, add_pair, 0)

    def chip_copy(d):
        return copy(pair_buf.at[chip_at(d)], chip_buf.at[d], chip_sem, (d,), grp, chip_at(d) * 2 + core)

    def run(lo, hi, act):
        def step(d, c):
            act(d)
            return c

        lax.fori_loop(lo, hi, step, 0)

    run(1, CHIPS, lambda d: chip_copy(d).start())
    run(1, CHIPS, lambda d: chip_copy(d).wait())

    total = pair_buf[chip]
    for d in range(1, CHIPS):
        total = total + chip_buf[d]
    own[...] = total * (1.0 / (POSITIONS * KEEP))

    def z_copy(d):
        to = lax.rem(grp + d, GRPS)
        return copy(own.at[pl.ds(z_start(to), ZROWS)], z_buf.at[d], z_sem, (d,), to, dev)

    run(1, GRPS, lambda d: z_copy(d).start())

    def all_copy(src, d, to_core):
        return copy(src, full.at[core, chip], all_sem, (to_core, d), grp, chip_at(d) * 2 + to_core)

    def all_recv(c, d):
        return pltpu.make_async_remote_copy(
            src_ref=own,
            dst_ref=full.at[c, chip_back(d)],
            send_sem=all_sem.at[0, 0, d],
            recv_sem=rx_sem(c, d),
            device_id=(grp, partner),
            device_id_type=MESH,
        )

    def rx_sem(c, d):
        return all_sem.at[1, c, d]

    def gather_copy(src, d, to_core):
        return pltpu.make_async_remote_copy(
            src_ref=src,
            dst_ref=full.at[core, chip],
            send_sem=all_sem.at[0, to_core, d],
            recv_sem=rx_sem(core, d),
            device_id=(grp, chip_at(d) * 2 + to_core),
            device_id_type=MESH,
        )

    run(1, CHIPS, lambda d: gather_copy(own, d, 0).start())

    @pl.when(core == 1)
    def _():
        gather_copy(own, 0, 0).start()

    @pl.when(core == 0)
    def _():
        full[0, chip] = own[...]

    run(1, GRPS, lambda d: z_copy(d).wait())
    total = own[pl.ds(z_start(grp), ZROWS), :]
    for d in range(1, GRPS):
        total = total + z_buf[d]
    z_sum[...] = total * (1.0 / GRPS)

    def m_copy(d):
        return copy(z_sum, z_all.at[grp], m_sem, (d,), lax.rem(grp + d, GRPS), dev)

    run(1, GRPS, lambda d: m_copy(d).start())
    z_all[grp] = z_sum[...]

    def m_recv(d):
        return copy(z_sum, z_all.at[lax.rem(grp + GRPS - d, GRPS)], m_sem, (d,), grp, partner)

    run(1, GRPS, lambda d: m_recv(d).wait_recv())
    run(1, GRPS, lambda d: m_copy(d).wait_send())
    for z in range(GRPS):
        at = (z * 15) // 7 * 8
        mean[at : at + ZROWS, :] = z_all[z]

    run(1, CHIPS, lambda d: gather_copy(mean, d, 1).start())

    @pl.when(core == 0)
    def _():
        gather_copy(mean, 0, 1).start()

    @pl.when(core == 1)
    def _():
        full[1, chip] = mean[...]

    def finish(d):
        all_recv(0, d).wait_recv()
        all_recv(1, d).wait_recv()
        gather_copy(own, d, 0).wait_send()
        gather_copy(mean, d, 1).wait_send()

    run(1, CHIPS, finish)

    @pl.when(core == 1)
    def _():
        all_recv(0, 0).wait_recv()
        gather_copy(own, 0, 0).wait_send()

    @pl.when(core == 0)
    def _():
        all_recv(1, 0).wait_recv()
        gather_copy(mean, 0, 1).wait_send()


def reduce_gram(gram):
    vmem = pl.BlockSpec(memory_space=pltpu.VMEM)
    dma = pltpu.SemaphoreType.DMA
    return pl.pallas_call(
        reduce_kernel,
        out_shape=jax.ShapeDtypeStruct((2, CHIPS, SHARD, NB), F32),
        in_specs=[pl.BlockSpec(memory_space=pltpu.HBM)],
        out_specs=vmem,
        scratch_shapes=[
            pltpu.VMEM((CHIPS, SHARD, NB), F32),
            pltpu.VMEM((CHIPS, SHARD, NB), F32),
            pltpu.VMEM((CHIPS, SHARD, NB), F32),
            pltpu.VMEM((SHARD, NB), F32),
            pltpu.VMEM((GRPS, ZROWS, NB), F32),
            pltpu.VMEM((ZROWS, NB), F32),
            pltpu.VMEM((GRPS, ZROWS, NB), F32),
            pltpu.VMEM((SHARD, NB), F32),
            dma,
            dma((2,)),
            dma((2, CHIPS)),
            dma((2, GRPS)),
            dma((2, GRPS)),
            dma((2, 2, CHIPS)),
        ],
        compiler_params=pltpu.CompilerParams(
            collective_id=0, has_side_effects=True, vmem_limit_bytes=61 << 20
        ),
        name="reduce_gram",
    )(gram.reshape(2, CHIPS, SHARD, NB))


def diag_factor(d):
    n = NB // 8
    lane = lax.broadcasted_iota(I32, (8, NB), 1)
    sub = lax.broadcasted_iota(I32, (8, NB), 0)
    t_rows = [d[8 * s : 8 * s + 8, :] for s in range(n)]
    e_rows = [jnp.where(lane == sub + 8 * s, 1.0, 0.0).astype(F32) for s in range(n)]
    r_out, e_out = [], []
    for s in range(n):
        c0 = 8 * s
        t, e = t_rows[s], e_rows[s]
        cols = [jnp.broadcast_to(t[:, c0 + j : c0 + j + 1], (8, NB)) for j in range(8)]
        b = {}
        for i in range(8):
            for j in range(i, 8):
                b[i, j] = jnp.broadcast_to(cols[j][i : i + 1, :], (8, NB))
        rows = [jnp.broadcast_to(t[j : j + 1, :], (8, NB)) for j in range(8)]
        extra = [jnp.broadcast_to(e[j : j + 1, :], (8, NB)) for j in range(8)]
        r_strip = e_strip = None
        for j in range(8):
            scale = lax.rsqrt(b[j, j])
            low = {k: b[j, k] * scale for k in range(j + 1, 8)}
            for i in range(j + 1, 8):
                for k in range(i, 8):
                    b[i, k] = b[i, k] - low[i] * low[k]
            rj, ej = rows[j] * scale, extra[j] * scale
            for i in range(j + 1, 8):
                rows[i] = rows[i] - low[i] * rj
                extra[i] = extra[i] - low[i] * ej
            r_strip = rj if j == 0 else jnp.where(sub == j, rj, r_strip)
            e_strip = ej if j == 0 else jnp.where(sub == j, ej, e_strip)
        r_out.append(r_strip)
        e_out.append(e_strip)
        if s == n - 1:
            break
        w = jnp.concatenate([r_strip, e_strip], axis=1)
        h = w.astype(BF16).astype(F32)
        rest = w - h
        m = rest.astype(BF16).astype(F32)
        q = rest - m
        lhs = jnp.concatenate([v[:, :NB] for v in (h, h, m, m, h, q)], axis=0).astype(BF16)
        rhs = jnp.concatenate([h, m, h, m, q, h], axis=0).astype(BF16)
        update = dot_t(lhs, rhs)
        for i in range(s + 1, n):
            t_rows[i] = t_rows[i] - update[8 * i : 8 * i + 8, :NB]
            e_rows[i] = e_rows[i] - update[8 * i : 8 * i + 8, NB:]
    return jnp.concatenate(r_out, axis=0), jnp.concatenate(e_out, axis=0)


def cholesky_kernel(g, out, a, r, d):
    for i in range(NBLK):
        for j in range(i, NBLK):
            at = packed(i, j) * NB
            a[i * NB : (i + 1) * NB, j * NB : (j + 1) * NB] = g[at : at + NB, :]
    row = lax.broadcasted_iota(I32, (NB, NB), 0)
    col = lax.broadcasted_iota(I32, (NB, NB), 1)
    d[...] = a[0:NB, 0:NB]

    def step(k, c):
        top, inverse = diag_factor(d[...])
        d[...] = jnp.where(row <= col, top, 0.0)
        hi, mid = split2(inverse)
        left = jnp.concatenate([hi, hi, mid], axis=1)
        for kk in range(NBLK):

            @pl.when(k == kk)
            def _():
                k0, k1 = kk * NB, (kk + 1) * NB
                r[k0:k1, k0:k1] = d[...]
                if kk:
                    r[k0:k1, 0:k0] = jnp.zeros((NB, k0), F32)
                if kk == NBLK - 1:
                    return
                hi, mid = split2(a[k0:k1, k1:])
                strip = dot_n(left, jnp.concatenate([hi, mid, hi], axis=0))
                r[k0:k1, k1:] = strip
                hi, mid = split2(strip)
                lhs = jnp.concatenate([hi, hi, mid], axis=0)
                rhs = jnp.concatenate([hi, mid, hi], axis=0)
                d[...] = a[k1 : k1 + NB, k1 : k1 + NB] - dot_t(lhs[:, :NB], rhs[:, :NB])
                for i in range((COLS - k1) // NB):
                    lo, hi_ = i * NB, (i + 1) * NB
                    if i:
                        a[k1 + lo : k1 + hi_, k1 + lo :] -= dot_t(lhs[:, lo:hi_], rhs[:, lo:])
                    elif kk < NBLK - 2:
                        a[k1 : k1 + NB, k1 + NB :] -= dot_t(lhs[:, :NB], rhs[:, NB:])

        return c

    lax.fori_loop(0, NBLK, step, 0)
    chip = lax.axis_index("dev") // 2
    out[...] = r[pl.ds(pl.multiple_of(chip * 64, 64), 64), :]


def cholesky_rows(full):
    vmem = pl.BlockSpec(memory_space=pltpu.VMEM)
    return pl.pallas_call(
        cholesky_kernel,
        out_shape=jax.ShapeDtypeStruct((2 * COLS // DEVS, COLS), F32),
        in_specs=[vmem],
        out_specs=vmem,
        scratch_shapes=[
            pltpu.VMEM((COLS, COLS), F32),
            pltpu.VMEM((COLS, COLS), F32),
            pltpu.VMEM((NB, NB), F32),
        ],
        compiler_params=pltpu.CompilerParams(vmem_limit_bytes=32 << 20),
        cost_estimate=pl.CostEstimate(flops=50_000_000_000, bytes_accessed=100_000_000, transcendentals=0),
        name="cholesky_rows",
    )(full.reshape(DEVS * SHARD, NB))


def place_kernel(order_in, counts_in, arrived, sketch, order, counts, stage, zero, tab_sem, in_sem, sem):
    me = lax.axis_index("dev")
    tables = [
        pltpu.make_async_copy(order_in, order, tab_sem.at[0]),
        pltpu.make_async_copy(counts_in, counts, tab_sem.at[1]),
    ]
    for table in tables:
        table.start()
    zero[...] = jnp.zeros_like(zero)
    for table in tables:
        table.wait()

    def add(e, c):
        return c + jnp.where(e < me, counts[0, e], 0)

    offset = lax.fori_loop(0, DEVS, add, jnp.int32(0))
    held = counts[0, me]

    def load(j):
        source = order[0, jnp.minimum(offset + j, POSITIONS - 1)] >> 4
        return pltpu.make_async_copy(arrived.at[source], stage.at[j], in_sem.at[j])

    def start(j, c):
        @pl.when(j < held)
        def _():
            load(j).start()

        @pl.when(j >= held)
        def _():
            pltpu.make_async_copy(zero, sketch.at[j], sem.at[j]).start()

        return c

    def store(j, c):
        @pl.when(j < held)
        def _():
            load(j).wait()
            pltpu.make_async_copy(stage.at[j], sketch.at[j], sem.at[j]).start()

        return c

    def wait(j, c):
        pltpu.make_async_copy(zero, sketch.at[j], sem.at[j]).wait()
        return c

    lax.fori_loop(0, DEVS, start, 0)
    lax.fori_loop(0, DEVS, store, 0)
    lax.fori_loop(0, DEVS, wait, 0)


def place(block_order, counts, arrived):
    hbm = pl.BlockSpec(memory_space=pltpu.HBM)
    return pl.pallas_call(
        place_kernel,
        out_shape=jax.ShapeDtypeStruct((DEVS, KEEP, COLS), F32),
        in_specs=[hbm] * 3,
        out_specs=hbm,
        scratch_shapes=[
            pltpu.SMEM((1, POSITIONS), I32),
            pltpu.SMEM((1, DEVS), I32),
            pltpu.VMEM((DEVS, KEEP, COLS), F32),
            pltpu.VMEM((KEEP, COLS), F32),
            pltpu.SemaphoreType.DMA((2,)),
            pltpu.SemaphoreType.DMA((DEVS,)),
            pltpu.SemaphoreType.DMA((DEVS,)),
        ],
        compiler_params=pltpu.CompilerParams(vmem_limit_bytes=16 << 20),
        name="place_slots",
    )(block_order, counts, arrived)


def body(matrix, block_order, counts, sign_bits, row_mask):
    send, gram = mix(matrix, block_order, counts, sign_bits, row_mask)
    full = reduce_gram(gram)
    send, full = lax.optimization_barrier((send, full))
    arrived = lax.all_to_all(send, "dev", split_axis=0, concat_axis=0, tiled=True)
    rows = cholesky_rows(full)
    half = rows.shape[0] // 2
    first = lax.rem(lax.axis_index("dev"), 2) == 0
    mine = jnp.where(first, rows[:half], rows[half:])
    other = jnp.where(first, rows[half:], rows[:half])
    other = lax.ppermute(other, "dev", [(d, d ^ 1) for d in range(DEVS)])
    sketch = place(block_order, counts, arrived)
    group_factor = jnp.where(first, mine, other)[None]
    factor = jnp.where(first, other, mine)
    return sketch.reshape(DEVS * KEEP, COLS), group_factor, factor


def solution(mesh):
    placed = (
        P(("grp", "dev"), None),
        P("grp", None),
        P("grp", None),
        P("grp", None, None),
        P("grp", None, None),
    )
    return jax.shard_map(
        body,
        mesh=mesh,
        in_specs=placed,
        out_specs=(P(("grp", "dev"), None), P("grp", "dev", None), P("dev", None)),
        check_vma=False,
    )
```

time: 944 us -> 143 us (0.15)
  waiting for transfers between devices: 388 us -> 0.99 us
  other arithmetic: 385 us -> 0.75 us
  Pallas kernels: 0 us -> 133 us
  matrix products: 73 us -> 0 us
  local copies, waits for them, and re-layouts: 59.1 us -> 0.02 us
  between operations: 25.2 us -> 0.87 us
    another operation x65 -> x0, other arithmetic: 346 us -> none  [the longest x31 173 us: body(): mean_upper = jnp.linalg.cholesky(mean_gram).T]
    all_to_all x1, waiting for transfers between devices: 226 us -> 0.01 us  [body(): lax.all_to_all(send, 'dev', split_axis=0, concat_axis=0, tiled=True)]
    psum x2 -> x0, waiting for transfers between devices: 161 us -> none  [the longest x1 161 us: body(): group_gram = lax.psum(partial_value, 'dev') / float(positions * KEEP)]
    pallas_call x0 -> x4, Pallas kernels: none -> 133 us  [the longest x1 65.3 us: reduce_gram(): pl.pallas_call(reduce_kernel, out_shape=jax.ShapeDtypeStruct((2, CHIPS, S...]
    another operation x28 -> x0, matrix products: 45.5 us -> none  [the longest x14 22.8 us: body(): group_upper = jnp.linalg.cholesky(group_gram).T]
    gather x7 -> x0, local copies, waits for them, and re-layouts: 29.1 us -> none  [the longest x1 14.3 us: body(): my_blocks = jnp.take(arrived, from_slot, axis=0)]
    dot_general x3 -> x0, matrix products: 27.5 us -> none  [the longest x1 14.9 us: gram_of(): jnp.einsum('kc,ke->ce', flat_rows, flat_rows, precision=lax.Precision.HIG...]
    div x4 -> x0, other arithmetic: 18.9 us -> none  [the longest x1 5.01 us: body(): mean_gram = lax.psum(group_gram, 'grp') / float(groups)]
  transfers between devices with their start and end apart: 3 -> 2, of which waited for: 2 -> 1; matrix products, arithmetic and copies ran while one was open for 19% -> 1% of each run, Pallas kernels for 0% -> 37%
where the time goes in v1:
time: 143 us; the launch traced here: 142 us
  Pallas kernels  133 us (93%)
  starting transfers between devices  5.64 us (4%)
    pallas_call x1, Pallas kernels, reduce_gram(): pl.pallas_call(reduce_kernel, out_shape=jax.ShapeDtypeStruct((2, CHIPS, S...  65.3 us
    pallas_call x1, Pallas kernels, cholesky_rows(): pl.pallas_call(cholesky_kernel, out_shape=jax.ShapeDtypeStruct((2 * COLS...  52.4 us
    pallas_call x1, Pallas kernels, mix(): pl.pallas_call(mix_kernel, out_shape=(jax.ShapeDtypeStruct((DEVS, KEEP, C...  12.3 us
    all_to_all x1, starting transfers between devices, body(): lax.all_to_all(send, 'dev', split_axis=0, concat_axis=0, tiled=True)  5.08 us
    pallas_call x1, Pallas kernels, place(): pl.pallas_call(place_kernel, out_shape=jax.ShapeDtypeStruct((DEVS, KEEP,...  3.51 us
  transfers between devices with their start and end apart: 2, of which 1 were waited for; matrix products, arithmetic and copies ran while one was open for 1% of the time, Pallas kernels for 37%

profile of v1, /device:TPU:1, one launch (start us, length us, event | category | flops | bytes accessed | tf_op | source)
XLA Modules:
  0.0 141.7 jit_solution(9104891402497514304)
XLA Ops:
  0.6 12.3 %mix_rows.1 = (f32[32,32,1024]{2,1,0:T(8,128)}, f32[4608,128]{1,0:T(8,128)}) custom-call(s32[1,512]{1,0:T(1,128)} %order_in.3, s32[1,32]{1,0:T(1,128)} %counts_in.3, f32[2048,1024]{1,0:T(8,128)} %matrix.1, s32[1,512,128]{2,1,0:T(8,128)} %sign_bits.1, s32[1,512,128]{2,1,0:T(8,128)} %row_mask.1), custom_call_target="tpu_custom_call" | custom-call | tf_op jit(solution)/shard_map/mix_rows/pallas_call | solution.py:130
  12.9 65.3 %reduce_gram.1 = f32[2,16,144,128]{3,2,1,0:T(8,128)} custom-call(f32[2,16,144,128]{3,2,1,0:T(8,128)} %bitcast.7), custom_call_target="tpu_custom_call" | custom-call | tf_op jit(solution)/shard_map/reduce_gram/pallas_call | solution.py:332
  78.2 0.0 copy-start
  78.2 5.1 %all-to-all-start = ((f32[32,32,1024]{2,1,0:T(8,128)}), f32[32,32,1024]{2,1,0:T(8,128)}, u32[]{:S(2)}, u32[]{:S(2)}) async-start(f32[32,32,1024]{2,1,0:T(8,128)} %get-tuple-element.9), calls=%async_computation | async-start | bytes 8388608 | tf_op jit(solution)/shard_map/all_to_all | solution.py:546
  83.3 0.0 copy-done
  83.3 0.0 copy-start.1
  83.4 0.0 copy-start.2
  83.4 52.4 %cholesky_rows.1 = f32[64,1024]{1,0:T(8,128)S(1)} custom-call(f32[4608,128]{1,0:T(8,128)S(1)} %bitcast.5), custom_call_target="tpu_custom_call" | custom-call | flops 49999998976 | bytes 100000000 | tf_op jit(solution)/shard_map/cholesky_rows/pallas_call | solution.py:455
  135.8 0.6 collective-permute-start
  136.4 1.0 collective-permute-done
  137.3 0.7 broadcast_select_fusion
  138.1 0.0 all-to-all-done.arrived
  138.1 0.0 copy-done.1
  138.1 0.0 copy-done.2
  138.1 3.5 %place_slots.1 = f32[32,32,1024]{2,1,0:T(8,128)} custom-call(s32[1,512]{1,0:T(1,128)S(1)} %copy-done.1, s32[1,32]{1,0:T(1,128)S(1)} %copy-done.2, f32[32,32,1024]{2,1,0:T(8,128)} %all-to-all-done.arrived), custom_call_target="tpu_custom_call" | custom-call | tf_op jit(solution)/shard_map/place_slots/pallas_call | solution.py:523
  (1 shorter events, 0.0 us)
Async XLA Ops:
  78.2 5.1 %copy-start = (f32[2,16,144,128]{3,2,1,0:T(8,128)S(1)}, f32[2,16,144,128]{3,2,1,0:T(8,128)}, u32[]{:S(2)}) copy-start(f32[2,16,144,128]{3,2,1,0:T(8,128)} %reduce_gram.1) | copy-start | bytes 7077892
  78.2 59.8 %all-to-all-start = ((f32[32,32,1024]{2,1,0:T(8,128)}), f32[32,32,1024]{2,1,0:T(8,128)}, u32[]{:S(2)}, u32[]{:S(2)}) async-start(f32[32,32,1024]{2,1,0:T(8,128)} %get-tuple-element.9), calls=%async_computation | async-start | bytes 8388608 | tf_op jit(solution)/shard_map/all_to_all | solution.py:546
  83.3 54.7 %copy-start.1 = (s32[1,512]{1,0:T(1,128)S(1)}, s32[1,512]{1,0:T(1,128)}, u32[]{:S(2)}) copy-start(s32[1,512]{1,0:T(1,128)} %order_in.3) | copy-start | bytes 6148
  83.4 54.7 %copy-start.2 = (s32[1,32]{1,0:T(1,128)S(1)}, s32[1,32]{1,0:T(1,128)}, u32[]{:S(2)}) copy-start(s32[1,32]{1,0:T(1,128)} %counts_in.3) | copy-start | bytes 388
  135.8 1.6 %collective-permute-start = (f32[32,1024]{1,0:T(8,128)S(1)}, f32[32,1024]{1,0:T(8,128)S(1)}, u32[]{:S(2)}, u32[]{:S(2)}) collective-permute-start(f32[32,1024]{1,0:T(8,128)S(1)} %slice_select_fusion), channel_id=1, source_target_pairs={{0,1},{1,0},{2,3},{3,2},{4,5},{5,4},{6,7},{7,6},{8,9},{9,8},{10,11... | collective-permute-start | bytes 393224 | tf_op jit(solution)/shard_map/ppermute | solution.py:552

commit v2 on v1

--- a/solution.py
+++ b/solution.py
@@ -19,6 +19,8 @@
 CHIPS = 16
 SHARD = NBLK * (NBLK + 1) // 2 * NB // DEVS
 ZROWS = 24
+HALF = SHARD // 2
+CUT = 40
 
 
 def packed(i, j):
@@ -156,20 +158,30 @@
     )(block_order, counts, matrix, sign_bits, row_mask)
 
 
-def reduce_kernel(g, full, mine, pair_buf, chip_buf, own, z_buf, z_sum, z_all, mean, own_sem, pair_sem, chip_sem, z_sem, m_sem, all_sem):
+def reduce_kernel(
+    g, full, mine, acc, fwd, got, fwd_p, fwd_m, got2, own, z_buf, z_sum, z_all, mean,
+    own_sem, pair_sem, rs_sem, z_sem, m_sem, swap_sem, ag_sem,
+):
     grp = lax.axis_index("grp")
     dev = lax.axis_index("dev")
     core = lax.rem(dev, 2)
     chip = dev // 2
     cx, cy = chip // 4, lax.rem(chip, 4)
-
-    def chip_at(d):
-        return lax.rem(cx + d // 4, 4) * 4 + lax.rem(cy + lax.rem(d, 4), 4)
-
-    def chip_back(d):
-        return lax.rem(cx + 4 - d // 4, 4) * 4 + lax.rem(cy + 4 - lax.rem(d, 4), 4)
-
-    def copy(src, dst, sem, at, to_grp, to_dev):
+    partner = chip * 2 + 1 - core
+    first = (cx, cy)
+    second = (cy, cx)
+
+    def mod4(i):
+        return lax.rem(i + 4, 4)
+
+    def neighbour(h, dim, step):
+        if (h + dim) % 2 == 0:
+            to = mod4(cx + step) * 4 + cy
+        else:
+            to = cx * 4 + mod4(cy + step)
+        return to * 2 + core
+
+    def copy(src, dst, sem, at, to_dev, to_grp=grp):
         return pltpu.make_async_remote_copy(
             src_ref=src,
             dst_ref=dst,
@@ -179,45 +191,18 @@
             device_id_type=MESH,
         )
 
+    sent = []
+
+    def send(*args):
+        c = copy(*args)
+        c.start()
+        sent.append(c)
+
+    def receive(dst, sem, at):
+        copy(dst, dst, sem, at, partner).wait_recv()
+
     def z_start(z):
         return pl.multiple_of((z * 15) // 7 * 8, 8)
-
-    partner = chip * 2 + 1 - core
-    keep = pltpu.make_async_copy(g.at[core], mine, own_sem)
-    keep.start()
-    barrier = pltpu.get_barrier_semaphore()
-
-    def greet(to_grp, to_dev):
-        pl.semaphore_signal(barrier, inc=1, device_id=(to_grp, to_dev), device_id_type=MESH)
-
-    greet(grp, partner)
-
-    def greet_chip(d, c):
-        greet(grp, chip_at(d) * 2)
-        greet(grp, chip_at(d) * 2 + 1)
-        return c
-
-    def greet_z(d, c):
-        greet(lax.rem(grp + d, GRPS), dev)
-        return c
-
-    lax.fori_loop(1, CHIPS, greet_chip, 0)
-    lax.fori_loop(1, GRPS, greet_z, 0)
-    pl.semaphore_wait(barrier, 1 + 2 * (CHIPS - 1) + GRPS - 1)
-
-    pair = copy(g.at[1 - core], pair_buf, pair_sem, (), grp, partner)
-    pair.start()
-    keep.wait()
-    pair.wait()
-
-    def add_pair(i, c):
-        pair_buf[i] = pair_buf[i] + mine[i]
-        return c
-
-    lax.fori_loop(0, CHIPS, add_pair, 0)
-
-    def chip_copy(d):
-        return copy(pair_buf.at[chip_at(d)], chip_buf.at[d], chip_sem, (d,), grp, chip_at(d) * 2 + core)
 
     def run(lo, hi, act):
         def step(d, c):
@@ -226,55 +211,98 @@
 
         lax.fori_loop(lo, hi, step, 0)
 
-    run(1, CHIPS, lambda d: chip_copy(d).start())
-    run(1, CHIPS, lambda d: chip_copy(d).wait())
-
-    total = pair_buf[chip]
-    for d in range(1, CHIPS):
-        total = total + chip_buf[d]
-    own[...] = total * (1.0 / (POSITIONS * KEEP))
+    keep = pltpu.make_async_copy(g.at[core], mine, own_sem)
+    keep.start()
+    barrier = pltpu.get_barrier_semaphore()
+
+    def greet(to_dev, to_grp=grp):
+        pl.semaphore_signal(barrier, inc=1, device_id=(to_grp, to_dev), device_id_type=MESH)
+
+    greet(partner)
+    for dim in range(2):
+        for step in (1, -1):
+            greet(neighbour(0, dim, step))
+    run(1, GRPS, lambda d: greet(dev, lax.rem(grp + d, GRPS)))
+    pl.semaphore_wait(barrier, 5 + GRPS - 1)
+
+    steps = (2, 1, -1, 0)
+    for i, step in enumerate(steps):
+        for h in range(2):
+            a = mod4(first[h] + step)
+            send(g.at[1 - core, h, a], acc.at[h, a], pair_sem, (h, i), partner)
+    keep.wait()
+
+    def pair_sum(i):
+        for h in range(2):
+            a = mod4(first[h] + steps[i])
+            receive(acc.at[h, a], pair_sem, (h, i))
+            acc[h, a] = acc[h, a] + mine[h, a]
+
+    lo, hi = pl.ds(0, 2), pl.ds(2, 2)
+    pair_sum(0)
+    for h in range(2):
+        u = first[h]
+        send(acc.at[h, mod4(u + 2), lo], fwd.at[h, 0], rs_sem, (h, 0), neighbour(h, 0, 1))
+        send(acc.at[h, mod4(u + 2), hi], fwd.at[h, 1], rs_sem, (h, 1), neighbour(h, 0, -1))
+    pair_sum(1)
+    for h in range(2):
+        send(acc.at[h, mod4(first[h] + 1), hi], got.at[h, 0, hi], rs_sem, (h, 2), neighbour(h, 0, 1))
+    pair_sum(2)
+    for h in range(2):
+        send(acc.at[h, mod4(first[h] - 1), lo], got.at[h, 1, lo], rs_sem, (h, 3), neighbour(h, 0, -1))
+    pair_sum(3)
+    for h in range(2):
+        up, down = mod4(first[h] + 1), mod4(first[h] - 1)
+        receive(fwd.at[h, 0], rs_sem, (h, 0))
+        acc[h, up, 0:2] = acc[h, up, 0:2] + fwd[h, 0]
+        send(acc.at[h, up, lo], got.at[h, 0, lo], rs_sem, (h, 4), neighbour(h, 0, 1))
+        receive(fwd.at[h, 1], rs_sem, (h, 1))
+        acc[h, down, 2:4] = acc[h, down, 2:4] + fwd[h, 1]
+        send(acc.at[h, down, hi], got.at[h, 1, hi], rs_sem, (h, 5), neighbour(h, 0, -1))
+    top, bottom = pl.ds(0, CUT), pl.ds(CUT, HALF - CUT)
+    for h in range(2):
+        u, v = first[h], second[h]
+        receive(got.at[h, 0, hi], rs_sem, (h, 2))
+        receive(got.at[h, 1, lo], rs_sem, (h, 3))
+        receive(got.at[h, 0, lo], rs_sem, (h, 4))
+        receive(got.at[h, 1, hi], rs_sem, (h, 5))
+        acc[h, u] = acc[h, u] + got[h, 0] + got[h, 1]
+        send(acc.at[h, u, mod4(v + 2), top], fwd_p.at[h], rs_sem, (h, 6), neighbour(h, 1, 1))
+        send(acc.at[h, u, mod4(v + 2), bottom], fwd_m.at[h], rs_sem, (h, 7), neighbour(h, 1, -1))
+        send(acc.at[h, u, mod4(v + 1), bottom], got2.at[h, 0, bottom], rs_sem, (h, 8), neighbour(h, 1, 1))
+        send(acc.at[h, u, mod4(v - 1), top], got2.at[h, 1, top], rs_sem, (h, 9), neighbour(h, 1, -1))
+    for h in range(2):
+        u, up, down = first[h], mod4(second[h] + 1), mod4(second[h] - 1)
+        receive(fwd_p.at[h], rs_sem, (h, 6))
+        acc[h, u, up, 0:CUT] = acc[h, u, up, 0:CUT] + fwd_p[h]
+        send(acc.at[h, u, up, top], got2.at[h, 0, top], rs_sem, (h, 10), neighbour(h, 1, 1))
+        receive(fwd_m.at[h], rs_sem, (h, 7))
+        acc[h, u, down, CUT:HALF] = acc[h, u, down, CUT:HALF] + fwd_m[h]
+        send(acc.at[h, u, down, bottom], got2.at[h, 1, bottom], rs_sem, (h, 11), neighbour(h, 1, -1))
+    for h in range(2):
+        receive(got2.at[h, 0, bottom], rs_sem, (h, 8))
+        receive(got2.at[h, 1, top], rs_sem, (h, 9))
+        receive(got2.at[h, 0, top], rs_sem, (h, 10))
+        receive(got2.at[h, 1, bottom], rs_sem, (h, 11))
+        total = acc[h, first[h], second[h]] + got2[h, 0] + got2[h, 1]
+        own[h * HALF : (h + 1) * HALF, :] = total * (1.0 / (POSITIONS * KEEP))
 
     def z_copy(d):
         to = lax.rem(grp + d, GRPS)
-        return copy(own.at[pl.ds(z_start(to), ZROWS)], z_buf.at[d], z_sem, (d,), to, dev)
+        return copy(own.at[pl.ds(z_start(to), ZROWS)], z_buf.at[d], z_sem, (d,), dev, to)
 
     run(1, GRPS, lambda d: z_copy(d).start())
 
-    def all_copy(src, d, to_core):
-        return copy(src, full.at[core, chip], all_sem, (to_core, d), grp, chip_at(d) * 2 + to_core)
-
-    def all_recv(c, d):
-        return pltpu.make_async_remote_copy(
-            src_ref=own,
-            dst_ref=full.at[c, chip_back(d)],
-            send_sem=all_sem.at[0, 0, d],
-            recv_sem=rx_sem(c, d),
-            device_id=(grp, partner),
-            device_id_type=MESH,
-        )
-
-    def rx_sem(c, d):
-        return all_sem.at[1, c, d]
-
-    def gather_copy(src, d, to_core):
-        return pltpu.make_async_remote_copy(
-            src_ref=src,
-            dst_ref=full.at[core, chip],
-            send_sem=all_sem.at[0, to_core, d],
-            recv_sem=rx_sem(core, d),
-            device_id=(grp, chip_at(d) * 2 + to_core),
-            device_id_type=MESH,
-        )
-
-    run(1, CHIPS, lambda d: gather_copy(own, d, 0).start())
+    def block(h):
+        return full.at[h, first[h], second[h], core]
+
+    def swap(src, h):
+        return copy(src.at[pl.ds(h * HALF, HALF)], block(h), swap_sem, (h,), partner)
 
     @pl.when(core == 1)
     def _():
-        gather_copy(own, 0, 0).start()
-
-    @pl.when(core == 0)
-    def _():
-        full[0, chip] = own[...]
+        for h in range(2):
+            swap(own, h).start()
 
     run(1, GRPS, lambda d: z_copy(d).wait())
     total = own[pl.ds(z_start(grp), ZROWS), :]
@@ -283,114 +311,169 @@
     z_sum[...] = total * (1.0 / GRPS)
 
     def m_copy(d):
-        return copy(z_sum, z_all.at[grp], m_sem, (d,), lax.rem(grp + d, GRPS), dev)
+        return copy(z_sum, z_all.at[grp], m_sem, (d,), dev, lax.rem(grp + d, GRPS))
 
     run(1, GRPS, lambda d: m_copy(d).start())
     z_all[grp] = z_sum[...]
 
-    def m_recv(d):
-        return copy(z_sum, z_all.at[lax.rem(grp + GRPS - d, GRPS)], m_sem, (d,), grp, partner)
-
-    run(1, GRPS, lambda d: m_recv(d).wait_recv())
-    run(1, GRPS, lambda d: m_copy(d).wait_send())
+    def m_receive(d):
+        receive(z_all.at[lax.rem(grp + GRPS - d, GRPS)], m_sem, (d,))
+
+    run(1, GRPS, m_receive)
     for z in range(GRPS):
         at = (z * 15) // 7 * 8
         mean[at : at + ZROWS, :] = z_all[z]
 
-    run(1, CHIPS, lambda d: gather_copy(mean, d, 1).start())
-
     @pl.when(core == 0)
     def _():
-        gather_copy(mean, 0, 1).start()
+        for h in range(2):
+            swap(mean, h).start()
+            full[h, first[h], second[h], 0] = own[h * HALF : (h + 1) * HALF, :]
 
     @pl.when(core == 1)
     def _():
-        full[1, chip] = mean[...]
-
-    def finish(d):
-        all_recv(0, d).wait_recv()
-        all_recv(1, d).wait_recv()
-        gather_copy(own, d, 0).wait_send()
-        gather_copy(mean, d, 1).wait_send()
-
-    run(1, CHIPS, finish)
-
-    @pl.when(core == 1)
-    def _():
-        all_recv(0, 0).wait_recv()
-        gather_copy(own, 0, 0).wait_send()
-
-    @pl.when(core == 0)
-    def _():
-        all_recv(1, 0).wait_recv()
-        gather_copy(mean, 0, 1).wait_send()
+        for h in range(2):
+            full[h, first[h], second[h], 1] = mean[h * HALF : (h + 1) * HALF, :]
+
+    for h in range(2):
+        receive(full.at[h, first[h], second[h], 1 - core], swap_sem, (h,))
+
+    def spread(piece, slot, h, dim):
+        send(piece, piece, ag_sem, (h, slot), neighbour(h, dim, 1))
+        send(piece, piece, ag_sem, (h, slot + 1), neighbour(h, dim, -1))
+
+    def forward(before, after, slot, h, dim):
+        receive(before, ag_sem, (h, slot))
+        receive(after, ag_sem, (h, slot + 1))
+        send(before.at[0], before.at[0], ag_sem, (h, slot + 2), neighbour(h, dim, 1))
+        send(after.at[1], after.at[1], ag_sem, (h, slot + 3), neighbour(h, dim, -1))
+
+    def last(opposite, slot, h):
+        receive(opposite.at[0], ag_sem, (h, slot + 2))
+        receive(opposite.at[1], ag_sem, (h, slot + 3))
+
+    def at(h, i, j):
+        return full.at[h, mod4(first[h] + i), mod4(second[h] + j)]
+
+    for h in range(2):
+        spread(at(h, 0, 0), 0, h, 1)
+    for h in range(2):
+        spread(at(h, 0, 0), 4, h, 0)
+    for h in range(2):
+        forward(at(h, 0, -1), at(h, 0, 1), 0, h, 1)
+    for h in range(2):
+        spread(at(h, 0, -1), 8, h, 0)
+        spread(at(h, 0, 1), 12, h, 0)
+    for h in range(2):
+        forward(at(h, -1, 0), at(h, 1, 0), 4, h, 0)
+        last(at(h, 0, 2), 0, h)
+        spread(at(h, 0, 2), 16, h, 0)
+    for j, slot in ((-1, 8), (1, 12), (2, 16)):
+        for h in range(2):
+            forward(at(h, -1, j), at(h, 1, j), slot, h, 0)
+    for j, slot in ((0, 4), (-1, 8), (1, 12), (2, 16)):
+        for h in range(2):
+            last(at(h, 2, j), slot, h)
+
+    run(1, GRPS, lambda d: m_copy(d).wait_send())
+    for h in range(2):
+        swap(own, h).wait_send()
+    for c in sent:
+        c.wait_send()
 
 
 def reduce_gram(gram):
-    vmem = pl.BlockSpec(memory_space=pltpu.VMEM)
     dma = pltpu.SemaphoreType.DMA
+    vmem = lambda *shape: pltpu.VMEM((*shape, NB), F32)
     return pl.pallas_call(
         reduce_kernel,
-        out_shape=jax.ShapeDtypeStruct((2, CHIPS, SHARD, NB), F32),
+        out_shape=jax.ShapeDtypeStruct((2, 4, 4, 2, HALF, NB), F32),
         in_specs=[pl.BlockSpec(memory_space=pltpu.HBM)],
-        out_specs=vmem,
+        out_specs=pl.BlockSpec(memory_space=pltpu.VMEM),
         scratch_shapes=[
-            pltpu.VMEM((CHIPS, SHARD, NB), F32),
-            pltpu.VMEM((CHIPS, SHARD, NB), F32),
-            pltpu.VMEM((CHIPS, SHARD, NB), F32),
-            pltpu.VMEM((SHARD, NB), F32),
-            pltpu.VMEM((GRPS, ZROWS, NB), F32),
-            pltpu.VMEM((ZROWS, NB), F32),
-            pltpu.VMEM((GRPS, ZROWS, NB), F32),
-            pltpu.VMEM((SHARD, NB), F32),
+            vmem(2, 4, 4, HALF),
+            vmem(2, 4, 4, HALF),
+            vmem(2, 2, 2, HALF),
+            vmem(2, 2, 4, HALF),
+            vmem(2, CUT),
+            vmem(2, HALF - CUT),
+            vmem(2, 2, HALF),
+            vmem(SHARD),
+            vmem(GRPS, ZROWS),
+            vmem(ZROWS),
+            vmem(GRPS, ZROWS),
+            vmem(SHARD),
             dma,
-            dma((2,)),
-            dma((2, CHIPS)),
+            dma((2, 2, 4)),
+            dma((2, 2, 12)),
             dma((2, GRPS)),
             dma((2, GRPS)),
-            dma((2, 2, CHIPS)),
+            dma((2, 2)),
+            dma((2, 2, 20)),
         ],
         compiler_params=pltpu.CompilerParams(
             collective_id=0, has_side_effects=True, vmem_limit_bytes=61 << 20
         ),
         name="reduce_gram",
-    )(gram.reshape(2, CHIPS, SHARD, NB))
+    )(gram.reshape(2, 2, 4, 4, HALF, NB))
 
 
 def diag_factor(d):
     n = NB // 8
     lane = lax.broadcasted_iota(I32, (8, NB), 1)
     sub = lax.broadcasted_iota(I32, (8, NB), 0)
+
+    def column(x, i):
+        return jnp.broadcast_to(x[:, i : i + 1], (8, NB))
+
+    def line(x, i):
+        return jnp.broadcast_to(x[i : i + 1, :], (8, NB))
+
     t_rows = [d[8 * s : 8 * s + 8, :] for s in range(n)]
     e_rows = [jnp.where(lane == sub + 8 * s, 1.0, 0.0).astype(F32) for s in range(n)]
     r_out, e_out = [], []
+    low, scale, r_lines, e_lines = {}, [], [], []
     for s in range(n):
         c0 = 8 * s
         t, e = t_rows[s], e_rows[s]
-        cols = [jnp.broadcast_to(t[:, c0 + j : c0 + j + 1], (8, NB)) for j in range(8)]
-        b = {}
-        for i in range(8):
-            for j in range(i, 8):
-                b[i, j] = jnp.broadcast_to(cols[j][i : i + 1, :], (8, NB))
-        rows = [jnp.broadcast_to(t[j : j + 1, :], (8, NB)) for j in range(8)]
-        extra = [jnp.broadcast_to(e[j : j + 1, :], (8, NB)) for j in range(8)]
+        cols = [column(t, c0 + j) for j in range(8)]
+        if s:
+            before = []
+            for j in range(8):
+                c = column(t_rows[s], c0 - 8 + j)
+                for m in range(j):
+                    c = c - before[m] * low[m, j]
+                before.append(c * scale[j])
+            for j in range(8):
+                c = before[j]
+                t = t - c * r_lines[j]
+                e = e - c * e_lines[j]
+                cols = [x - c * line(c, k) for k, x in enumerate(cols)]
+        b = {(i, j): line(cols[j], i) for i in range(8) for j in range(i, 8)}
+        rows = [line(t, j) for j in range(8)]
+        extra = [line(e, j) for j in range(8)]
+        low, scale, r_lines, e_lines = {}, [], [], []
         r_strip = e_strip = None
         for j in range(8):
-            scale = lax.rsqrt(b[j, j])
-            low = {k: b[j, k] * scale for k in range(j + 1, 8)}
+            q = lax.rsqrt(b[j, j])
+            scale.append(q)
+            for k in range(j + 1, 8):
+                low[j, k] = b[j, k] * q
             for i in range(j + 1, 8):
                 for k in range(i, 8):
-                    b[i, k] = b[i, k] - low[i] * low[k]
-            rj, ej = rows[j] * scale, extra[j] * scale
+                    b[i, k] = b[i, k] - low[j, i] * low[j, k]
+            rj, ej = rows[j] * q, extra[j] * q
+            r_lines.append(rj)
+            e_lines.append(ej)
             for i in range(j + 1, 8):
-                rows[i] = rows[i] - low[i] * rj
-                extra[i] = extra[i] - low[i] * ej
+                rows[i] = rows[i] - low[j, i] * rj
+                extra[i] = extra[i] - low[j, i] * ej
             r_strip = rj if j == 0 else jnp.where(sub == j, rj, r_strip)
             e_strip = ej if j == 0 else jnp.where(sub == j, ej, e_strip)
         r_out.append(r_strip)
         e_out.append(e_strip)
-        if s == n - 1:
-            break
+        if s + 2 >= n:
+            continue
         w = jnp.concatenate([r_strip, e_strip], axis=1)
         h = w.astype(BF16).astype(F32)
         rest = w - h
@@ -399,7 +482,7 @@
         lhs = jnp.concatenate([v[:, :NB] for v in (h, h, m, m, h, q)], axis=0).astype(BF16)
         rhs = jnp.concatenate([h, m, h, m, q, h], axis=0).astype(BF16)
         update = dot_t(lhs, rhs)
-        for i in range(s + 1, n):
+        for i in range(s + 2, n):
             t_rows[i] = t_rows[i] - update[8 * i : 8 * i + 8, :NB]
             e_rows[i] = e_rows[i] - update[8 * i : 8 * i + 8, NB:]
     return jnp.concatenate(r_out, axis=0), jnp.concatenate(e_out, axis=0)
@@ -409,7 +492,14 @@
     for i in range(NBLK):
         for j in range(i, NBLK):
             at = packed(i, j) * NB
-            a[i * NB : (i + 1) * NB, j * NB : (j + 1) * NB] = g[at : at + NB, :]
+            row, end = 0, NB
+            while row < end:
+                shard, start = divmod(at + row, HALF)
+                size = min(HALF - start, end - row)
+                half, chip = shard // CHIPS % 2, shard % CHIPS
+                part = g[half, chip // 4, chip % 4, shard // (2 * CHIPS), start : start + size, :]
+                a[i * NB + row : i * NB + row + size, j * NB : (j + 1) * NB] = part
+                row += size
     row = lax.broadcasted_iota(I32, (NB, NB), 0)
     col = lax.broadcasted_iota(I32, (NB, NB), 1)
     d[...] = a[0:NB, 0:NB]
@@ -465,7 +555,7 @@
         compiler_params=pltpu.CompilerParams(vmem_limit_bytes=32 << 20),
         cost_estimate=pl.CostEstimate(flops=50_000_000_000, bytes_accessed=100_000_000, transcendentals=0),
         name="cholesky_rows",
-    )(full.reshape(DEVS * SHARD, NB))
+    )(full)
 
 
 def place_kernel(order_in, counts_in, arrived, sketch, order, counts, stage, zero, tab_sem, in_sem, sem):

time: 143 us -> 136 us (0.951)
  Pallas kernels: 133 us -> 105 us
  waiting for transfers between devices: 0.99 us -> 20.6 us
    pallas_call x1, Pallas kernels: 52.4 us -> 30.2 us  [cholesky_rows(): pl.pallas_call(cholesky_kernel, out_shape=jax.ShapeDtypeStruct((2 * COLS...]
    all_to_all x1, waiting for transfers between devices: 0.01 us -> 19.6 us  [body(): lax.all_to_all(send, 'dev', split_axis=0, concat_axis=0, tiled=True)]
    pallas_call x1, Pallas kernels: 65.3 us -> 58.6 us  [reduce_gram(): pl.pallas_call(reduce_kernel, out_shape=jax.ShapeDtypeStruct((2, 4, 4, 2,...]
  transfers between devices with their start and end apart: 2 -> 2, of which waited for: 1 -> 2; matrix products, arithmetic and copies ran while one was open for 1% -> 1% of each run, Pallas kernels for 37% -> 23%
where the time goes in v2:
time: 136 us; the launch traced here: 134 us
  Pallas kernels  105 us (77%)
  waiting for transfers between devices  20.6 us (15%)
  starting transfers between devices  6.43 us (5%)
    pallas_call x1, Pallas kernels, reduce_gram(): pl.pallas_call(reduce_kernel, out_shape=jax.ShapeDtypeStruct((2, 4, 4, 2,...  58.6 us
    pallas_call x1, Pallas kernels, cholesky_rows(): pl.pallas_call(cholesky_kernel, out_shape=jax.ShapeDtypeStruct((2 * COLS...  30.2 us
    all_to_all x1, waiting for transfers between devices, body(): lax.all_to_all(send, 'dev', split_axis=0, concat_axis=0, tiled=True)  19.6 us
    pallas_call x1, Pallas kernels, mix(): pl.pallas_call(mix_kernel, out_shape=(jax.ShapeDtypeStruct((DEVS, KEEP, C...  12.3 us
    all_to_all x1, starting transfers between devices, body(): lax.all_to_all(send, 'dev', split_axis=0, concat_axis=0, tiled=True)  5.85 us
    pallas_call x1, Pallas kernels, place(): pl.pallas_call(place_kernel, out_shape=jax.ShapeDtypeStruct((DEVS, KEEP,...  4.08 us
  transfers between devices with their start and end apart: 2, of which 2 were waited for; matrix products, arithmetic and copies ran while one was open for 1% of the time, Pallas kernels for 23%

profile of v2, /device:TPU:1, one launch (start us, length us, event | category | flops | bytes accessed | tf_op | source)
XLA Modules:
  0.0 133.8 jit_solution(1095010031033906429)
XLA Ops:
  0.6 12.3 %mix_rows.1 = (f32[32,32,1024]{2,1,0:T(8,128)}, f32[4608,128]{1,0:T(8,128)}) custom-call(s32[1,512]{1,0:T(1,128)} %order_in.3, s32[1,32]{1,0:T(1,128)} %counts_in.3, f32[2048,1024]{1,0:T(8,128)} %matrix.1, s32[1,512,128]{2,1,0:T(8,128)} %sign_bits.1, s32[1,512,128]{2,1,0:T(8,128)} %row_mask.1), custom_call_target="tpu_custom_call" | custom-call | tf_op jit(solution)/shard_map/mix_rows/pallas_call | solution.py:132
  12.9 58.6 %reduce_gram.1.g = f32[2,4,4,2,72,128]{5,4,3,2,1,0:T(8,128)} custom-call(f32[2,2,4,4,72,128]{5,4,3,2,1,0:T(8,128)} %bitcast.5), custom_call_target="tpu_custom_call" | custom-call | tf_op jit(solution)/shard_map/reduce_gram/pallas_call | solution.py:388
  71.5 0.0 copy-start
  71.5 5.9 %all-to-all-start = ((f32[32,32,1024]{2,1,0:T(8,128)}), f32[32,32,1024]{2,1,0:T(8,128)}, u32[]{:S(2)}, u32[]{:S(2)}) async-start(f32[32,32,1024]{2,1,0:T(8,128)} %get-tuple-element.9), calls=%async_computation | async-start | bytes 8388608 | tf_op jit(solution)/shard_map/all_to_all | solution.py:636
  77.4 0.0 copy-done
  77.4 0.0 copy-start.1
  77.4 0.0 copy-start.2
  77.4 30.2 %cholesky_rows.1 = f32[64,1024]{1,0:T(8,128)S(1)} custom-call(f32[2,4,4,2,72,128]{5,4,3,2,1,0:T(8,128)S(1)} %copy-done), custom_call_target="tpu_custom_call" | custom-call | flops 49999998976 | bytes 100000000 | tf_op jit(solution)/shard_map/cholesky_rows/pallas_call | solution.py:545
  107.7 0.6 collective-permute-start
  108.3 1.0 collective-permute-done
  109.3 0.7 broadcast_select_fusion
  110.0 19.6 %all-to-all-done.arrived = f32[32,32,1024]{2,1,0:T(8,128)} async-done(((f32[32,32,1024]{2,1,0:T(8,128)}), f32[32,32,1024]{2,1,0:T(8,128)}, u32[]{:S(2)}, u32[]{:S(2)}) %all-to-all-start) | async-done | bytes 4194336 | tf_op jit(solution)/shard_map/all_to_all | solution.py:636
  129.6 0.0 copy-done.1
  129.6 0.0 copy-done.2
  129.6 4.1 %place_slots.1 = f32[32,32,1024]{2,1,0:T(8,128)} custom-call(s32[1,512]{1,0:T(1,128)S(1)} %copy-done.1, s32[1,32]{1,0:T(1,128)S(1)} %copy-done.2, f32[32,32,1024]{2,1,0:T(8,128)} %all-to-all-done.arrived), custom_call_target="tpu_custom_call" | custom-call | tf_op jit(solution)/shard_map/place_slots/pallas_call | solution.py:613
  (1 shorter events, 0.0 us)
Async XLA Ops:
  71.5 5.9 %copy-start = (f32[2,4,4,2,72,128]{5,4,3,2,1,0:T(8,128)S(1)}, f32[2,4,4,2,72,128]{5,4,3,2,1,0:T(8,128)}, u32[]{:S(2)}) copy-start(f32[2,4,4,2,72,128]{5,4,3,2,1,0:T(8,128)} %reduce_gram.1.g) | copy-start | bytes 7077892
  71.5 58.1 %all-to-all-start = ((f32[32,32,1024]{2,1,0:T(8,128)}), f32[32,32,1024]{2,1,0:T(8,128)}, u32[]{:S(2)}, u32[]{:S(2)}) async-start(f32[32,32,1024]{2,1,0:T(8,128)} %get-tuple-element.9), calls=%async_computation | async-start | bytes 8388608 | tf_op jit(solution)/shard_map/all_to_all | solution.py:636
  77.4 52.2 %copy-start.1 = (s32[1,512]{1,0:T(1,128)S(1)}, s32[1,512]{1,0:T(1,128)}, u32[]{:S(2)}) copy-start(s32[1,512]{1,0:T(1,128)} %order_in.3) | copy-start | bytes 6148
  77.4 52.2 %copy-start.2 = (s32[1,32]{1,0:T(1,128)S(1)}, s32[1,32]{1,0:T(1,128)}, u32[]{:S(2)}) copy-start(s32[1,32]{1,0:T(1,128)} %counts_in.3) | copy-start | bytes 388
  107.7 1.6 %collective-permute-start = (f32[32,1024]{1,0:T(8,128)S(1)}, f32[32,1024]{1,0:T(8,128)S(1)}, u32[]{:S(2)}, u32[]{:S(2)}) collective-permute-start(f32[32,1024]{1,0:T(8,128)S(1)} %slice_select_fusion), channel_id=1, source_target_pairs={{0,1},{1,0},{2,3},{3,2},{4,5},{5,4},{6,7},{7,6},{8,9},{9,8},{10,11... | collective-permute-start | bytes 393224 | tf_op jit(solution)/shard_map/ppermute | solution.py:642

commit v3 on v2

--- a/solution.py
+++ b/solution.py
@@ -21,6 +21,14 @@
 ZROWS = 24
 HALF = SHARD // 2
 CUT = 40
+EARLY = 8
+
+OTHERS = [
+    (x, y, c)
+    for c in range(2)
+    for x, y in ((1, 0), (0, 1), (3, 0), (0, 3), (1, 1), (3, 3), (1, 3), (3, 1), (2, 0), (0, 2), (2, 1), (1, 2), (2, 3), (3, 2), (2, 2))
+] + [(0, 0, 1)]
+GAPS = (14, 0, 0, 9, 8)
 
 
 def packed(i, j):
@@ -40,7 +48,7 @@
     return lax.dot_general(a, b, (((1,), (0,)), ((), ())), preferred_element_type=F32)
 
 
-def mix_kernel(order_in, counts_in, matrix, sign_bits, row_mask, send, gram, x, order, counts, signs, masks, s_rows, s_hi, s_mid, gram_v, place, tab_sem, in_sem, out_sem, gram_sem):
+def mix_kernel(order_in, counts_in, matrix, sign_bits, row_mask, send_a, send_b, gram, x, order, counts, signs, masks, s_rows, s_hi, s_mid, gram_v, place, tab_sem, in_sem, out_sem, gram_sem):
     me = lax.axis_index("dev")
 
     def fetch(k):
@@ -107,9 +115,11 @@
         hi, mid = split2(mixed)
         s_hi[rows, :] = hi
         s_mid[rows, :] = mid
-        out = pltpu.make_async_copy(s_rows.at[rows], send.at[owners[k]], out_sem.at[k])
-        out.start()
-        outs.append(out)
+        cut = k * KEEP + EARLY
+        for i, part, send in ((0, pl.ds(k * KEEP, EARLY), send_a), (1, pl.ds(cut, KEEP - EARLY), send_b)):
+            out = pltpu.make_async_copy(s_rows.at[part], send.at[owners[k]], out_sem.at[k, i])
+            out.start()
+            outs.append(out)
 
     for i in range(NBLK):
         a, b = i * NB, (i + 1) * NB
@@ -132,11 +142,12 @@
     return pl.pallas_call(
         mix_kernel,
         out_shape=(
-            jax.ShapeDtypeStruct((DEVS, KEEP, COLS), F32),
+            jax.ShapeDtypeStruct((DEVS, EARLY, COLS), F32),
+            jax.ShapeDtypeStruct((DEVS, KEEP - EARLY, COLS), F32),
             jax.ShapeDtypeStruct((DEVS * SHARD, NB), F32),
         ),
         in_specs=[hbm] * 5,
-        out_specs=(hbm, hbm),
+        out_specs=(hbm, hbm, hbm),
         scratch_shapes=[
             pltpu.VMEM((PER * BLOCK, COLS), F32),
             pltpu.SMEM((1, POSITIONS), I32),
@@ -150,7 +161,7 @@
             pltpu.SMEM((PER + 1,), I32),
             pltpu.SemaphoreType.DMA((4,)),
             pltpu.SemaphoreType.DMA((PER,)),
-            pltpu.SemaphoreType.DMA((PER,)),
+            pltpu.SemaphoreType.DMA((PER, 2)),
             pltpu.SemaphoreType.DMA((NBLK,)),
         ],
         compiler_params=pltpu.CompilerParams(vmem_limit_bytes=62 << 20),
@@ -159,8 +170,8 @@
 
 
 def reduce_kernel(
-    g, full, mine, acc, fwd, got, fwd_p, fwd_m, got2, own, z_buf, z_sum, z_all, mean,
-    own_sem, pair_sem, rs_sem, z_sem, m_sem, swap_sem, ag_sem,
+    g, blocks, full, arrived, mine, acc, fwd, got, fwd_p, fwd_m, got2, own, z_buf, z_sum, z_all, mean,
+    own_sem, pair_sem, rs_sem, z_sem, m_sem, swap_sem, ag_sem, all_sem, stay_sem,
 ):
     grp = lax.axis_index("grp")
     dev = lax.axis_index("dev")
@@ -174,12 +185,11 @@
     def mod4(i):
         return lax.rem(i + 4, 4)
 
+    def at_offset(dx, dy, flip=0):
+        return (mod4(cx + dx) * 4 + mod4(cy + dy)) * 2 + lax.rem(core + flip, 2)
+
     def neighbour(h, dim, step):
-        if (h + dim) % 2 == 0:
-            to = mod4(cx + step) * 4 + cy
-        else:
-            to = cx * 4 + mod4(cy + step)
-        return to * 2 + core
+        return at_offset(step, 0) if (h + dim) % 2 == 0 else at_offset(0, step)
 
     def copy(src, dst, sem, at, to_dev, to_grp=grp):
         return pltpu.make_async_remote_copy(
@@ -218,18 +228,29 @@
     def greet(to_dev, to_grp=grp):
         pl.semaphore_signal(barrier, inc=1, device_id=(to_grp, to_dev), device_id_type=MESH)
 
-    greet(partner)
-    for dim in range(2):
-        for step in (1, -1):
-            greet(neighbour(0, dim, step))
+    for others in OTHERS:
+        greet(at_offset(*others))
     run(1, GRPS, lambda d: greet(dev, lax.rem(grp + d, GRPS)))
-    pl.semaphore_wait(barrier, 5 + GRPS - 1)
+    pl.semaphore_wait(barrier, len(OTHERS) + GRPS - 1)
+
+    def block_copy(i):
+        to = at_offset(*OTHERS[i])
+        return copy(blocks.at[to], arrived.at[dev], all_sem, (i,), to)
+
+    pending = list(range(len(OTHERS)))
+
+    def fill(count):
+        for _ in range(min(count, len(pending))):
+            block_copy(pending.pop(0)).start()
 
     steps = (2, 1, -1, 0)
     for i, step in enumerate(steps):
         for h in range(2):
             a = mod4(first[h] + step)
             send(g.at[1 - core, h, a], acc.at[h, a], pair_sem, (h, i), partner)
+    stay = pltpu.make_async_copy(blocks.at[dev], arrived.at[dev], stay_sem)
+    stay.start()
+    fill(GAPS[0])
     keep.wait()
 
     def pair_sum(i):
@@ -259,6 +280,7 @@
         receive(fwd.at[h, 1], rs_sem, (h, 1))
         acc[h, down, 2:4] = acc[h, down, 2:4] + fwd[h, 1]
         send(acc.at[h, down, hi], got.at[h, 1, hi], rs_sem, (h, 5), neighbour(h, 0, -1))
+    fill(GAPS[1])
     top, bottom = pl.ds(0, CUT), pl.ds(CUT, HALF - CUT)
     for h in range(2):
         u, v = first[h], second[h]
@@ -279,6 +301,7 @@
         receive(fwd_m.at[h], rs_sem, (h, 7))
         acc[h, u, down, CUT:HALF] = acc[h, u, down, CUT:HALF] + fwd_m[h]
         send(acc.at[h, u, down, bottom], got2.at[h, 1, bottom], rs_sem, (h, 11), neighbour(h, 1, -1))
+    fill(GAPS[2])
     for h in range(2):
         receive(got2.at[h, 0, bottom], rs_sem, (h, 8))
         receive(got2.at[h, 1, top], rs_sem, (h, 9))
@@ -299,10 +322,70 @@
     def swap(src, h):
         return copy(src.at[pl.ds(h * HALF, HALF)], block(h), swap_sem, (h,), partner)
 
+    def spreads(i, h):
+        def at(i, j):
+            return full.at[h, mod4(first[h] + i), mod4(second[h] + j)]
+
+        def both(piece, slot, dim):
+            return [(piece, slot, dim, 1), (piece, slot + 1, dim, -1)]
+
+        def on(before, after, slot, dim):
+            return [(before.at[0], slot + 2, dim, 1), (after.at[1], slot + 3, dim, -1)]
+
+        if i == 0:
+            return both(at(0, 0), 0, 1) + both(at(0, 0), 4, 0)
+        if i == 1:
+            return on(at(0, -1), at(0, 1), 0, 1) + both(at(0, -1), 8, 0) + both(at(0, 1), 12, 0)
+        if i == 2:
+            return on(at(-1, 0), at(1, 0), 4, 0) + both(at(0, 2), 16, 0)
+        return [x for j, slot in ((-1, 8), (1, 12), (2, 16)) for x in on(at(-1, j), at(1, j), slot, 0)]
+
+    def needs(i, h):
+        def at(i, j):
+            return full.at[h, mod4(first[h] + i), mod4(second[h] + j)]
+
+        if i == 0:
+            return []
+        if i == 1:
+            return [(at(0, -1), 0), (at(0, 1), 1)]
+        if i == 2:
+            return [(at(-1, 0), 4), (at(1, 0), 5), (at(0, 2).at[0], 2), (at(0, 2).at[1], 3)]
+        if i == 3:
+            return [x for j, slot in ((-1, 8), (1, 12), (2, 16)) for x in ((at(-1, j), slot), (at(1, j), slot + 1))]
+        return [
+            x
+            for j, slot in ((0, 4), (-1, 8), (1, 12), (2, 16))
+            for x in ((at(2, j).at[0], slot + 2), (at(2, j).at[1], slot + 3))
+        ]
+
+    def leave(piece, slot, h, dim, step):
+        return copy(piece, piece, ag_sem, (h, slot), neighbour(h, dim, step))
+
+    def stage(i):
+        for h in range(2):
+            for piece, slot in needs(i, h):
+                receive(piece, ag_sem, (h, slot))
+            if i < 4:
+                for piece, slot, dim, step in spreads(i, h):
+                    leave(piece, slot, h, dim, step).start()
+
+    def begin(src):
+        for h in range(2):
+            full[h, first[h], second[h], core] = src[h * HALF : (h + 1) * HALF, :]
+        for h in range(2):
+            receive(full.at[h, first[h], second[h], 1 - core], swap_sem, (h,))
+        stage(0)
+
     @pl.when(core == 1)
     def _():
         for h in range(2):
             swap(own, h).start()
+
+    fill(GAPS[3])
+
+    @pl.when(core == 0)
+    def _():
+        begin(own)
 
     run(1, GRPS, lambda d: z_copy(d).wait())
     total = own[pl.ds(z_start(grp), ZROWS), :]
@@ -315,81 +398,61 @@
 
     run(1, GRPS, lambda d: m_copy(d).start())
     z_all[grp] = z_sum[...]
+    fill(GAPS[4])
+
+    @pl.when(core == 0)
+    def _():
+        stage(1)
 
     def m_receive(d):
         receive(z_all.at[lax.rem(grp + GRPS - d, GRPS)], m_sem, (d,))
 
     run(1, GRPS, m_receive)
     for z in range(GRPS):
-        at = (z * 15) // 7 * 8
-        mean[at : at + ZROWS, :] = z_all[z]
+        start = (z * 15) // 7 * 8
+        mean[start : start + ZROWS, :] = z_all[z]
 
     @pl.when(core == 0)
     def _():
         for h in range(2):
             swap(mean, h).start()
-            full[h, first[h], second[h], 0] = own[h * HALF : (h + 1) * HALF, :]
 
     @pl.when(core == 1)
     def _():
-        for h in range(2):
-            full[h, first[h], second[h], 1] = mean[h * HALF : (h + 1) * HALF, :]
-
-    for h in range(2):
-        receive(full.at[h, first[h], second[h], 1 - core], swap_sem, (h,))
-
-    def spread(piece, slot, h, dim):
-        send(piece, piece, ag_sem, (h, slot), neighbour(h, dim, 1))
-        send(piece, piece, ag_sem, (h, slot + 1), neighbour(h, dim, -1))
-
-    def forward(before, after, slot, h, dim):
-        receive(before, ag_sem, (h, slot))
-        receive(after, ag_sem, (h, slot + 1))
-        send(before.at[0], before.at[0], ag_sem, (h, slot + 2), neighbour(h, dim, 1))
-        send(after.at[1], after.at[1], ag_sem, (h, slot + 3), neighbour(h, dim, -1))
-
-    def last(opposite, slot, h):
-        receive(opposite.at[0], ag_sem, (h, slot + 2))
-        receive(opposite.at[1], ag_sem, (h, slot + 3))
-
-    def at(h, i, j):
-        return full.at[h, mod4(first[h] + i), mod4(second[h] + j)]
-
-    for h in range(2):
-        spread(at(h, 0, 0), 0, h, 1)
-    for h in range(2):
-        spread(at(h, 0, 0), 4, h, 0)
-    for h in range(2):
-        forward(at(h, 0, -1), at(h, 0, 1), 0, h, 1)
-    for h in range(2):
-        spread(at(h, 0, -1), 8, h, 0)
-        spread(at(h, 0, 1), 12, h, 0)
-    for h in range(2):
-        forward(at(h, -1, 0), at(h, 1, 0), 4, h, 0)
-        last(at(h, 0, 2), 0, h)
-        spread(at(h, 0, 2), 16, h, 0)
-    for j, slot in ((-1, 8), (1, 12), (2, 16)):
-        for h in range(2):
-            forward(at(h, -1, j), at(h, 1, j), slot, h, 0)
-    for j, slot in ((0, 4), (-1, 8), (1, 12), (2, 16)):
-        for h in range(2):
-            last(at(h, 2, j), slot, h)
+        begin(mean)
+        stage(1)
+
+    fill(len(OTHERS))
+    stage(2)
+    stage(3)
+    stage(4)
 
     run(1, GRPS, lambda d: m_copy(d).wait_send())
     for h in range(2):
         swap(own, h).wait_send()
+        for i in range(4):
+            for piece, slot, dim, step in spreads(i, h):
+                leave(piece, slot, h, dim, step).wait_send()
     for c in sent:
         c.wait_send()
-
-
-def reduce_gram(gram):
+    for i in range(len(OTHERS)):
+        dx, dy, flip = OTHERS[i]
+        copy(blocks.at[dev], arrived.at[at_offset(-dx, -dy, flip)], all_sem, (i,), partner).wait_recv()
+        block_copy(i).wait_send()
+    stay.wait()
+
+
+def reduce_gram(gram, blocks):
     dma = pltpu.SemaphoreType.DMA
     vmem = lambda *shape: pltpu.VMEM((*shape, NB), F32)
     return pl.pallas_call(
         reduce_kernel,
-        out_shape=jax.ShapeDtypeStruct((2, 4, 4, 2, HALF, NB), F32),
-        in_specs=[pl.BlockSpec(memory_space=pltpu.HBM)],
-        out_specs=pl.BlockSpec(memory_space=pltpu.VMEM),
+        out_shape=(
+            jax.ShapeDtypeStruct((2, 4, 4, 2, HALF, NB), F32),
+            jax.ShapeDtypeStruct(blocks.shape, F32),
+        ),
+        in_specs=[pl.BlockSpec(memory_space=pltpu.HBM)] * 2,
+        out_specs=(pl.BlockSpec(memory_space=pltpu.VMEM), pl.BlockSpec(memory_space=pltpu.HBM)),
         scratch_shapes=[
             vmem(2, 4, 4, HALF),
             vmem(2, 4, 4, HALF),
@@ -410,12 +473,14 @@
             dma((2, GRPS)),
             dma((2, 2)),
             dma((2, 2, 20)),
+            dma((2, len(OTHERS))),
+            dma,
         ],
         compiler_params=pltpu.CompilerParams(
             collective_id=0, has_side_effects=True, vmem_limit_bytes=61 << 20
         ),
         name="reduce_gram",
-    )(gram.reshape(2, 2, 4, 4, HALF, NB))
+    )(gram.reshape(2, 2, 4, 4, HALF, NB), blocks)
 
 
 def diag_factor(d):
@@ -558,7 +623,7 @@
     )(full)
 
 
-def place_kernel(order_in, counts_in, arrived, sketch, order, counts, stage, zero, tab_sem, in_sem, sem):
+def place_kernel(order_in, counts_in, arrived_a, arrived_b, sketch, order, counts, stage, zero, tab_sem, in_sem, sem):
     me = lax.axis_index("dev")
     tables = [
         pltpu.make_async_copy(order_in, order, tab_sem.at[0]),
@@ -578,12 +643,16 @@
 
     def load(j):
         source = order[0, jnp.minimum(offset + j, POSITIONS - 1)] >> 4
-        return pltpu.make_async_copy(arrived.at[source], stage.at[j], in_sem.at[j])
+        return (
+            pltpu.make_async_copy(arrived_a.at[source], stage.at[j, pl.ds(0, EARLY)], in_sem.at[j, 0]),
+            pltpu.make_async_copy(arrived_b.at[source], stage.at[j, pl.ds(EARLY, KEEP - EARLY)], in_sem.at[j, 1]),
+        )
 
     def start(j, c):
         @pl.when(j < held)
         def _():
-            load(j).start()
+            for part in load(j):
+                part.start()
 
         @pl.when(j >= held)
         def _():
@@ -594,7 +663,8 @@
     def store(j, c):
         @pl.when(j < held)
         def _():
-            load(j).wait()
+            for part in load(j):
+                part.wait()
             pltpu.make_async_copy(stage.at[j], sketch.at[j], sem.at[j]).start()
 
         return c
@@ -608,12 +678,12 @@
     lax.fori_loop(0, DEVS, wait, 0)
 
 
-def place(block_order, counts, arrived):
+def place(block_order, counts, arrived_a, arrived_b):
     hbm = pl.BlockSpec(memory_space=pltpu.HBM)
     return pl.pallas_call(
         place_kernel,
         out_shape=jax.ShapeDtypeStruct((DEVS, KEEP, COLS), F32),
-        in_specs=[hbm] * 3,
+        in_specs=[hbm] * 4,
         out_specs=hbm,
         scratch_shapes=[
             pltpu.SMEM((1, POSITIONS), I32),
@@ -621,26 +691,26 @@
             pltpu.VMEM((DEVS, KEEP, COLS), F32),
             pltpu.VMEM((KEEP, COLS), F32),
             pltpu.SemaphoreType.DMA((2,)),
-            pltpu.SemaphoreType.DMA((DEVS,)),
+            pltpu.SemaphoreType.DMA((DEVS, 2)),
             pltpu.SemaphoreType.DMA((DEVS,)),
         ],
-        compiler_params=pltpu.CompilerParams(vmem_limit_bytes=16 << 20),
+        compiler_params=pltpu.CompilerParams(vmem_limit_bytes=62 << 20),
         name="place_slots",
-    )(block_order, counts, arrived)
+    )(block_order, counts, arrived_a, arrived_b)
 
 
 def body(matrix, block_order, counts, sign_bits, row_mask):
-    send, gram = mix(matrix, block_order, counts, sign_bits, row_mask)
-    full = reduce_gram(gram)
-    send, full = lax.optimization_barrier((send, full))
-    arrived = lax.all_to_all(send, "dev", split_axis=0, concat_axis=0, tiled=True)
+    early, late, gram = mix(matrix, block_order, counts, sign_bits, row_mask)
+    full, early = reduce_gram(gram, early)
+    late, full = lax.optimization_barrier((late, full))
+    late = lax.all_to_all(late, "dev", split_axis=0, concat_axis=0, tiled=True)
     rows = cholesky_rows(full)
     half = rows.shape[0] // 2
     first = lax.rem(lax.axis_index("dev"), 2) == 0
     mine = jnp.where(first, rows[:half], rows[half:])
     other = jnp.where(first, rows[half:], rows[:half])
     other = lax.ppermute(other, "dev", [(d, d ^ 1) for d in range(DEVS)])
-    sketch = place(block_order, counts, arrived)
+    sketch = place(block_order, counts, early, late)
     group_factor = jnp.where(first, mine, other)[None]
     factor = jnp.where(first, other, mine)
     return sketch.reshape(DEVS * KEEP, COLS), group_factor, factor

time: 136 us -> 126 us (0.926); the launches traced: 134 us -> 125 us
  waiting for transfers between devices: 20.6 us -> 7.87 us
  Pallas kernels: 105 us -> 111 us
  starting transfers between devices: 6.43 us -> 5.02 us
    all_to_all x1, waiting for transfers between devices: 19.6 us -> 6.54 us  [body(): late = lax.all_to_all(late, 'dev', split_axis=0, concat_axis=0, tiled=True)]
    pallas_call x2, Pallas kernels: 70.9 us -> 76.9 us  [the longest x1 64.4 us: reduce_gram(): pl.pallas_call(reduce_kernel, out_shape=(jax.ShapeDtypeStruct((2, 4, 4, 2...]
  transfers between devices with their start and end apart: 2 -> 2, of which waited for: 2 -> 2; matrix products, arithmetic and copies ran while one was open for 1% -> 1% of each run, Pallas kernels for 23% -> 24%
where the time goes in v3:
time: 126 us; the launch traced here: 125 us
  Pallas kernels  111 us (88%)
  waiting for transfers between devices  7.87 us (6%)
  starting transfers between devices  5.02 us (4%)
    pallas_call x1, Pallas kernels, reduce_gram(): pl.pallas_call(reduce_kernel, out_shape=(jax.ShapeDtypeStruct((2, 4, 4, 2...  64.4 us
    pallas_call x1, Pallas kernels, cholesky_rows(): pl.pallas_call(cholesky_kernel, out_shape=jax.ShapeDtypeStruct((2 * COLS...  30.2 us
    pallas_call x1, Pallas kernels, mix(): pl.pallas_call(mix_kernel, out_shape=(jax.ShapeDtypeStruct((DEVS, EARLY,...  12.4 us
    all_to_all x1, waiting for transfers between devices, body(): late = lax.all_to_all(late, 'dev', split_axis=0, concat_axis=0, tiled=True)  6.54 us
    all_to_all x1, starting transfers between devices, body(): late = lax.all_to_all(late, 'dev', split_axis=0, concat_axis=0, tiled=True)  4.93 us
    pallas_call x1, Pallas kernels, place(): pl.pallas_call(place_kernel, out_shape=jax.ShapeDtypeStruct((DEVS, KEEP,...  3.76 us
  transfers between devices with their start and end apart: 2, of which 2 were waited for; matrix products, arithmetic and copies ran while one was open for 1% of the time, Pallas kernels for 24%

profile of v3, /device:TPU:1, one launch (start us, length us, event | category | flops | bytes accessed | tf_op | source)
XLA Modules:
  0.0 125.4 jit_solution(4072669113273936144)
XLA Ops:
  0.6 12.4 %mix_rows.1 = (f32[32,8,1024]{2,1,0:T(8,128)}, f32[32,24,1024]{2,1,0:T(8,128)}, f32[4608,128]{1,0:T(8,128)}) custom-call(s32[1,512]{1,0:T(1,128)} %order_in.3, s32[1,32]{1,0:T(1,128)} %counts_in.3, f32[2048,1024]{1,0:T(8,128)} %matrix.1, s32[1,512,128]{2,1,0:T(8,128)} %sign_bits.1, s32[1,512,128]{2,1,0:T(8,128)} %row_mask.1), custom_call_target="tpu_custom_call" | custom-call | tf_op jit(solution)/shard_map/mix_rows/pallas_call | solution.py:142
  13.1 64.4 %reduce_gram.1 = (f32[2,4,4,2,72,128]{5,4,3,2,1,0:T(8,128)}, f32[32,8,1024]{2,1,0:T(8,128)}) custom-call(f32[2,2,4,4,72,128]{5,4,3,2,1,0:T(8,128)} %bitcast.5, f32[32,8,1024]{2,1,0:T(8,128)} %get-tuple-element.11.blocks), custom_call_target="tpu_custom_call" | custom-call | tf_op jit(solution)/shard_map/reduce_gram/pallas_call | solution.py:448
  77.5 0.0 copy-start
  77.5 4.9 %all-to-all-start = ((f32[32,24,1024]{2,1,0:T(8,128)}), f32[32,24,1024]{2,1,0:T(8,128)}, u32[]{:S(2)}, u32[]{:S(2)}) async-start(f32[32,24,1024]{2,1,0:T(8,128)} %get-tuple-element.15), calls=%async_computation | async-start | bytes 6291456 | tf_op jit(solution)/shard_map/all_to_all | solution.py:706
  82.5 0.0 copy-done
  82.5 30.2 %cholesky_rows.1 = f32[64,1024]{1,0:T(8,128)S(1)} custom-call(f32[2,4,4,2,72,128]{5,4,3,2,1,0:T(8,128)S(1)} %copy-done), custom_call_target="tpu_custom_call" | custom-call | flops 49999998976 | bytes 100000000 | tf_op jit(solution)/shard_map/cholesky_rows/pallas_call | solution.py:610
  112.7 0.1 collective-permute-start
  112.8 1.3 %collective-permute-done = f32[32,1024]{1,0:T(8,128)S(1)} collective-permute-done((f32[32,1024]{1,0:T(8,128)S(1)}, f32[32,1024]{1,0:T(8,128)S(1)}, u32[]{:S(2)}, u32[]{:S(2)}) %collective-permute-start) | collective-permute-done | bytes 131104 | tf_op jit(solution)/shard_map/ppermute | solution.py:712
  114.2 0.7 broadcast_select_fusion
  114.9 6.5 %all-to-all-done.arrived_b = f32[32,24,1024]{2,1,0:T(8,128)} async-done(((f32[32,24,1024]{2,1,0:T(8,128)}), f32[32,24,1024]{2,1,0:T(8,128)}, u32[]{:S(2)}, u32[]{:S(2)}) %all-to-all-start) | async-done | bytes 3145760 | tf_op jit(solution)/shard_map/all_to_all | solution.py:706
  121.4 3.8 %place_slots.1 = f32[32,32,1024]{2,1,0:T(8,128)} custom-call(s32[1,512]{1,0:T(1,128)} %order_in.3, s32[1,32]{1,0:T(1,128)} %counts_in.3, f32[32,8,1024]{2,1,0:T(8,128)} %get-tuple-element.12.arrived_a, f32[32,24,1024]{2,1,0:T(8,128)} %all-to-all-done.arrived_b), custom_call_target="tpu_custom_call" | custom-call | tf_op jit(solution)/shard_map/place_slots/pallas_call | solution.py:683
  (1 shorter events, 0.0 us)
Async XLA Ops:
  77.5 5.0 %copy-start = (f32[2,4,4,2,72,128]{5,4,3,2,1,0:T(8,128)S(1)}, f32[2,4,4,2,72,128]{5,4,3,2,1,0:T(8,128)}, u32[]{:S(2)}) copy-start(f32[2,4,4,2,72,128]{5,4,3,2,1,0:T(8,128)} %get-tuple-element.16.g) | copy-start | bytes 7077892
  77.5 43.9 %all-to-all-start = ((f32[32,24,1024]{2,1,0:T(8,128)}), f32[32,24,1024]{2,1,0:T(8,128)}, u32[]{:S(2)}, u32[]{:S(2)}) async-start(f32[32,24,1024]{2,1,0:T(8,128)} %get-tuple-element.15), calls=%async_computation | async-start | bytes 6291456 | tf_op jit(solution)/shard_map/all_to_all | solution.py:706
  112.7 1.4 %collective-permute-start = (f32[32,1024]{1,0:T(8,128)S(1)}, f32[32,1024]{1,0:T(8,128)S(1)}, u32[]{:S(2)}, u32[]{:S(2)}) collective-permute-start(f32[32,1024]{1,0:T(8,128)S(1)} %slice_select_fusion), channel_id=1, source_target_pairs={{0,1},{1,0},{2,3},{3,2},{4,5},{5,4},{6,7},{7,6},{8,9},{9,8},{10,11... | collective-permute-start | bytes 393224 | tf_op jit(solution)/shard_map/ppermute | solution.py:712

commit v4 on v3

--- a/solution.py
+++ b/solution.py
@@ -28,11 +28,20 @@
     for c in range(2)
     for x, y in ((1, 0), (0, 1), (3, 0), (0, 3), (1, 1), (3, 3), (1, 3), (3, 1), (2, 0), (0, 2), (2, 1), (1, 2), (2, 3), (3, 2), (2, 2))
 ] + [(0, 0, 1)]
-GAPS = (14, 0, 0, 9, 8)
+GAPS = (1, 0, 0, 12, 11)
 
 
 def packed(i, j):
     return i * NBLK - i * (i - 1) // 2 + (j - i)
+
+
+def pieces(block):
+    row = 0
+    while row < NB:
+        shard, start = divmod(block * NB + row, HALF)
+        size = min(HALF - start, NB - row)
+        yield row, size, (shard // 32, shard // 16 % 2, shard // 4 % 4, shard % 4), start
+        row += size
 
 
 def split2(x):
@@ -48,7 +57,7 @@
     return lax.dot_general(a, b, (((1,), (0,)), ((), ())), preferred_element_type=F32)
 
 
-def mix_kernel(order_in, counts_in, matrix, sign_bits, row_mask, send_a, send_b, gram, x, order, counts, signs, masks, s_rows, s_hi, s_mid, gram_v, place, tab_sem, in_sem, out_sem, gram_sem):
+def mix_kernel(order_in, counts_in, matrix, sign_bits, row_mask, send_a, send_b, kept, x, order, counts, signs, masks, s_rows, owner_v, place, tab_sem, in_sem, out_sem):
     me = lax.axis_index("dev")
 
     def fetch(k):
@@ -65,20 +74,17 @@
     tables[0].wait()
     tables[1].wait()
 
-    def find(p, carry):
-        b = order[0, p]
-        place[jnp.where((b >> 4) == me, b & 15, PER)] = p
-        return carry
-
-    lax.fori_loop(0, POSITIONS, find, 0, unroll=8)
-    pos = [place[k] for k in range(PER)]
-
-    def count(e, carry):
-        run, owners = carry
-        run = run + counts[0, e]
-        return run, tuple(o + (p >= run).astype(I32) for o, p in zip(owners, pos))
-
-    _, owners = lax.fori_loop(0, DEVS, count, (jnp.int32(0), (jnp.int32(0),) * PER))
+    block = lax.broadcasted_iota(I32, (PER, POSITIONS), 0) + me * PER
+    hit = jnp.where(order[...] == block, 1.0, 0.0)
+    where = lax.broadcasted_iota(I32, (PER, POSITIONS), 1).astype(F32)
+    pos = jnp.sum(hit * where, axis=1, keepdims=True)
+    earlier = lax.broadcasted_iota(I32, (DEVS, DEVS), 0) <= lax.broadcasted_iota(I32, (DEVS, DEVS), 1)
+    held = jnp.broadcast_to(counts[...].astype(F32), (PER, DEVS))
+    ends = dot_n(held.astype(BF16), jnp.where(earlier, 1.0, 0.0).astype(BF16))
+    owner = jnp.sum(jnp.where(ends <= pos, 1.0, 0.0), axis=1, keepdims=True)
+    owner_v[...] = jnp.broadcast_to(owner, (PER, BLOCK)).astype(I32)
+    owned = pltpu.make_async_copy(owner_v, place, tab_sem.at[4])
+    owned.start()
 
     row = lax.broadcasted_iota(I32, (BLOCK, BLOCK), 0)
     col = lax.broadcasted_iota(I32, (BLOCK, BLOCK), 1)
@@ -89,9 +95,10 @@
     upto = jnp.where(row <= col, 1.0, 0.0).astype(BF16)
     tables[2].wait()
     tables[3].wait()
-    mask = jnp.concatenate([masks[0, pl.ds(p, 1), :] for p in pos], axis=0).astype(F32)
-    sign = jnp.concatenate([signs[0, pl.ds(p, 1), :] for p in pos], axis=0)
-    sign = (1 - 2 * sign).astype(F32)
+    table = jnp.concatenate([masks[0], signs[0]], axis=1).astype(F32).astype(BF16)
+    both = dot_n(hit.astype(BF16), table)
+    mask = both[:, :BLOCK]
+    sign = 1.0 - 2.0 * both[:, BLOCK:]
     running = dot_n(mask.astype(BF16), upto).astype(I32)
     nth = lax.broadcasted_iota(I32, (KEEP, BLOCK), 0) + 1
     chosen = [
@@ -106,32 +113,21 @@
         block = x[k * BLOCK : (k + 1) * BLOCK, :]
         hi = block.astype(BF16)
         rest = block - hi.astype(F32)
-        mid = rest.astype(BF16)
-        low = (rest - mid.astype(F32)).astype(BF16)
-        mixed = dot_n(t, hi) + dot_n(t, mid) + dot_n(t, low)
+        mixed = dot_n(t, hi) + dot_n(t, rest.astype(BF16))
         mixed = mixed * float(BLOCK) ** -0.5
         rows = slice(k * KEEP, (k + 1) * KEEP)
         s_rows[rows, :] = mixed
-        hi, mid = split2(mixed)
-        s_hi[rows, :] = hi
-        s_mid[rows, :] = mid
+        out = pltpu.make_async_copy(s_rows.at[pl.ds(k * KEEP, KEEP)], kept.at[pl.ds(k * KEEP, KEEP)], out_sem.at[k, 2])
+        out.start()
+        outs.append(out)
+        if k == 0:
+            owned.wait()
         cut = k * KEEP + EARLY
         for i, part, send in ((0, pl.ds(k * KEEP, EARLY), send_a), (1, pl.ds(cut, KEEP - EARLY), send_b)):
-            out = pltpu.make_async_copy(s_rows.at[part], send.at[owners[k]], out_sem.at[k, i])
+            out = pltpu.make_async_copy(s_rows.at[part], send.at[place[k, 0]], out_sem.at[k, i])
             out.start()
             outs.append(out)
 
-    for i in range(NBLK):
-        a, b = i * NB, (i + 1) * NB
-        block = dot_t(s_hi[:, a:b], s_hi[:, a:]) + dot_t(s_hi[:, a:b], s_mid[:, a:])
-        block = block + dot_t(s_mid[:, a:b], s_hi[:, a:])
-        for j in range(i, NBLK):
-            at = packed(i, j) * NB
-            gram_v[at : at + NB, :] = block[:, (j - i) * NB : (j - i + 1) * NB]
-        rows = pl.ds(packed(i, i) * NB, (NBLK - i) * NB)
-        out = pltpu.make_async_copy(gram_v.at[rows], gram.at[rows], gram_sem.at[i])
-        out.start()
-        outs.append(out)
     for out in outs:
         out.wait()
 
@@ -144,25 +140,22 @@
         out_shape=(
             jax.ShapeDtypeStruct((DEVS, EARLY, COLS), F32),
             jax.ShapeDtypeStruct((DEVS, KEEP - EARLY, COLS), F32),
-            jax.ShapeDtypeStruct((DEVS * SHARD, NB), F32),
+            jax.ShapeDtypeStruct((rows, COLS), F32),
         ),
         in_specs=[hbm] * 5,
         out_specs=(hbm, hbm, hbm),
         scratch_shapes=[
             pltpu.VMEM((PER * BLOCK, COLS), F32),
-            pltpu.SMEM((1, POSITIONS), I32),
-            pltpu.SMEM((1, DEVS), I32),
+            pltpu.VMEM((1, POSITIONS), I32),
+            pltpu.VMEM((1, DEVS), I32),
             pltpu.VMEM((1, POSITIONS, BLOCK), I32),
             pltpu.VMEM((1, POSITIONS, BLOCK), I32),
             pltpu.VMEM((rows, COLS), F32),
-            pltpu.VMEM((rows, COLS), BF16),
-            pltpu.VMEM((rows, COLS), BF16),
-            pltpu.VMEM((DEVS * SHARD, NB), F32),
-            pltpu.SMEM((PER + 1,), I32),
-            pltpu.SemaphoreType.DMA((4,)),
+            pltpu.VMEM((PER, BLOCK), I32),
+            pltpu.SMEM((PER, BLOCK), I32),
+            pltpu.SemaphoreType.DMA((5,)),
             pltpu.SemaphoreType.DMA((PER,)),
-            pltpu.SemaphoreType.DMA((PER, 2)),
-            pltpu.SemaphoreType.DMA((NBLK,)),
+            pltpu.SemaphoreType.DMA((PER, 3)),
         ],
         compiler_params=pltpu.CompilerParams(vmem_limit_bytes=62 << 20),
         name="mix_rows",
@@ -170,7 +163,7 @@
 
 
 def reduce_kernel(
-    g, blocks, full, arrived, mine, acc, fwd, got, fwd_p, fwd_m, got2, own, z_buf, z_sum, z_all, mean,
+    kept, blocks, full, arrived, rows, s_hi, s_mid, g, acc, fwd, got, fwd_p, fwd_m, got2, own, z_buf, z_sum, z_all, mean,
     own_sem, pair_sem, rs_sem, z_sem, m_sem, swap_sem, ag_sem, all_sem, stay_sem,
 ):
     grp = lax.axis_index("grp")
@@ -221,7 +214,7 @@
 
         lax.fori_loop(lo, hi, step, 0)
 
-    keep = pltpu.make_async_copy(g.at[core], mine, own_sem)
+    keep = pltpu.make_async_copy(kept, rows, own_sem)
     keep.start()
     barrier = pltpu.get_barrier_semaphore()
 
@@ -231,7 +224,6 @@
     for others in OTHERS:
         greet(at_offset(*others))
     run(1, GRPS, lambda d: greet(dev, lax.rem(grp + d, GRPS)))
-    pl.semaphore_wait(barrier, len(OTHERS) + GRPS - 1)
 
     def block_copy(i):
         to = at_offset(*OTHERS[i])
@@ -243,21 +235,43 @@
         for _ in range(min(count, len(pending))):
             block_copy(pending.pop(0)).start()
 
+    keep.wait()
+    hi, mid = split2(rows[...])
+    s_hi[...] = hi
+    s_mid[...] = mid
     steps = (2, 1, -1, 0)
-    for i, step in enumerate(steps):
-        for h in range(2):
-            a = mod4(first[h] + step)
-            send(g.at[1 - core, h, a], acc.at[h, a], pair_sem, (h, i), partner)
+
+    def pair_copy(h, a):
+        return copy(g.at[1 - core, h, a], acc.at[h, a], pair_sem, (h, a), partner)
+
     stay = pltpu.make_async_copy(blocks.at[dev], arrived.at[dev], stay_sem)
     stay.start()
-    fill(GAPS[0])
-    keep.wait()
+    gone = 0
+    for i in range(NBLK):
+        left = slice(i * NB, (i + 1) * NB)
+        band = dot_t(s_hi[:, left], s_hi[:, i * NB :]) + dot_t(s_hi[:, left], s_mid[:, i * NB :])
+        band = band + dot_t(s_mid[:, left], s_hi[:, i * NB :])
+        for j in range(i, NBLK):
+            for row, size, (core_, half, x, y), start in pieces(packed(i, j)):
+                part = band[row : row + size, (j - i) * NB : (j - i + 1) * NB]
+                g[core_, half, x, y, start : start + size, :] = part
+        if i == 0:
+            pl.semaphore_wait(barrier, len(OTHERS) + GRPS - 1)
+        while gone < 16 and (gone + 1) * 4 * HALF <= (packed(i, NBLK - 1) + 1) * NB:
+            core_, half, x = gone // 8, gone // 4 % 2, gone % 4
+
+            @pl.when(core != core_)
+            def _():
+                pair_copy(half, x).start()
+
+            gone += 1
+        fill(GAPS[0])
 
     def pair_sum(i):
         for h in range(2):
             a = mod4(first[h] + steps[i])
-            receive(acc.at[h, a], pair_sem, (h, i))
-            acc[h, a] = acc[h, a] + mine[h, a]
+            receive(acc.at[h, a], pair_sem, (h, a))
+            acc[h, a] = acc[h, a] + g[core, h, a]
 
     lo, hi = pl.ds(0, 2), pl.ds(2, 2)
     pair_sum(0)
@@ -435,6 +449,9 @@
                 leave(piece, slot, h, dim, step).wait_send()
     for c in sent:
         c.wait_send()
+    for h in range(2):
+        for a in range(4):
+            pair_copy(h, a).wait_send()
     for i in range(len(OTHERS)):
         dx, dy, flip = OTHERS[i]
         copy(blocks.at[dev], arrived.at[at_offset(-dx, -dy, flip)], all_sem, (i,), partner).wait_recv()
@@ -442,7 +459,7 @@
     stay.wait()
 
 
-def reduce_gram(gram, blocks):
+def reduce_gram(kept, blocks):
     dma = pltpu.SemaphoreType.DMA
     vmem = lambda *shape: pltpu.VMEM((*shape, NB), F32)
     return pl.pallas_call(
@@ -454,7 +471,10 @@
         in_specs=[pl.BlockSpec(memory_space=pltpu.HBM)] * 2,
         out_specs=(pl.BlockSpec(memory_space=pltpu.VMEM), pl.BlockSpec(memory_space=pltpu.HBM)),
         scratch_shapes=[
-            vmem(2, 4, 4, HALF),
+            pltpu.VMEM(kept.shape, F32),
+            pltpu.VMEM(kept.shape, BF16),
+            pltpu.VMEM(kept.shape, BF16),
+            vmem(2, 2, 4, 4, HALF),
             vmem(2, 4, 4, HALF),
             vmem(2, 2, 2, HALF),
             vmem(2, 2, 4, HALF),
@@ -480,7 +500,7 @@
             collective_id=0, has_side_effects=True, vmem_limit_bytes=61 << 20
         ),
         name="reduce_gram",
-    )(gram.reshape(2, 2, 4, 4, HALF, NB), blocks)
+    )(kept, blocks)
 
 
 def diag_factor(d):
@@ -556,15 +576,9 @@
 def cholesky_kernel(g, out, a, r, d):
     for i in range(NBLK):
         for j in range(i, NBLK):
-            at = packed(i, j) * NB
-            row, end = 0, NB
-            while row < end:
-                shard, start = divmod(at + row, HALF)
-                size = min(HALF - start, end - row)
-                half, chip = shard // CHIPS % 2, shard % CHIPS
-                part = g[half, chip // 4, chip % 4, shard // (2 * CHIPS), start : start + size, :]
+            for row, size, (core_, half, x, y), start in pieces(packed(i, j)):
+                part = g[half, x, y, core_, start : start + size, :]
                 a[i * NB + row : i * NB + row + size, j * NB : (j + 1) * NB] = part
-                row += size
     row = lax.broadcasted_iota(I32, (NB, NB), 0)
     col = lax.broadcasted_iota(I32, (NB, NB), 1)
     d[...] = a[0:NB, 0:NB]
@@ -700,8 +714,8 @@
 
 
 def body(matrix, block_order, counts, sign_bits, row_mask):
-    early, late, gram = mix(matrix, block_order, counts, sign_bits, row_mask)
-    full, early = reduce_gram(gram, early)
+    early, late, kept = mix(matrix, block_order, counts, sign_bits, row_mask)
+    full, early = reduce_gram(kept, early)
     late, full = lax.optimization_barrier((late, full))
     late = lax.all_to_all(late, "dev", split_axis=0, concat_axis=0, tiled=True)
     rows = cholesky_rows(full)

time: 126 us -> 123 us (0.976)
  Pallas kernels: 111 us -> 107 us
    pallas_call x1, Pallas kernels: 12.4 us -> 8.84 us  [mix(): pl.pallas_call(mix_kernel, out_shape=(jax.ShapeDtypeStruct((DEVS, EARLY,...]
    pallas_call x1, Pallas kernels: 64.4 us -> 62.8 us  [reduce_gram(): pl.pallas_call(reduce_kernel, out_shape=(jax.ShapeDtypeStruct((2, 4, 4, 2...]
    pallas_call x1, Pallas kernels: 3.76 us -> 5.19 us  [place(): pl.pallas_call(place_kernel, out_shape=jax.ShapeDtypeStruct((DEVS, KEEP,...]
  transfers between devices with their start and end apart: 2 -> 2, of which waited for: 2 -> 2; matrix products, arithmetic and copies ran while one was open for 1% -> 1% of each run, Pallas kernels for 24% -> 25%
where the time goes in v4:
time: 123 us
  Pallas kernels  107 us (87%)
  waiting for transfers between devices  8.25 us (7%)
  starting transfers between devices  6.18 us (5%)
    pallas_call x1, Pallas kernels, reduce_gram(): pl.pallas_call(reduce_kernel, out_shape=(jax.ShapeDtypeStruct((2, 4, 4, 2...  62.8 us
    pallas_call x1, Pallas kernels, cholesky_rows(): pl.pallas_call(cholesky_kernel, out_shape=jax.ShapeDtypeStruct((2 * COLS...  30.2 us
    pallas_call x1, Pallas kernels, mix(): pl.pallas_call(mix_kernel, out_shape=(jax.ShapeDtypeStruct((DEVS, EARLY,...  8.84 us
    all_to_all x1, waiting for transfers between devices, body(): late = lax.all_to_all(late, 'dev', split_axis=0, concat_axis=0, tiled=True)  7.26 us
    all_to_all x1, starting transfers between devices, body(): late = lax.all_to_all(late, 'dev', split_axis=0, concat_axis=0, tiled=True)  5.63 us
    pallas_call x1, Pallas kernels, place(): pl.pallas_call(place_kernel, out_shape=jax.ShapeDtypeStruct((DEVS, KEEP,...  5.19 us
  transfers between devices with their start and end apart: 2, of which 2 were waited for; matrix products, arithmetic and copies ran while one was open for 1% of the time, Pallas kernels for 25%

profile of v4, /device:TPU:1, one launch (start us, length us, event | category | flops | bytes accessed | tf_op | source)
XLA Modules:
  0.0 123.1 jit_solution(2870053198286465103)
XLA Ops:
  0.6 8.8 %mix_rows.1 = (f32[32,8,1024]{2,1,0:T(8,128)}, f32[32,24,1024]{2,1,0:T(8,128)}, f32[512,1024]{1,0:T(8,128)}) custom-call(s32[1,512]{1,0:T(1,128)} %order_in.3, s32[1,32]{1,0:T(1,128)} %counts_in.3, f32[2048,1024]{1,0:T(8,128)} %matrix.1, s32[1,512,128]{2,1,0:T(8,128)} %sign_bits.1, s32[1,512,128]{2,1,0:T(8,128)} %row_mask.1), custom_call_target="tpu_custom_call" | custom-call | tf_op jit(solution)/shard_map/mix_rows/pallas_call | solution.py:138
  9.5 62.8 %reduce_gram.1 = (f32[2,4,4,2,72,128]{5,4,3,2,1,0:T(8,128)}, f32[32,8,1024]{2,1,0:T(8,128)}) custom-call(f32[512,1024]{1,0:T(8,128)} %get-tuple-element.10.kept, f32[32,8,1024]{2,1,0:T(8,128)} %get-tuple-element.11.blocks), custom_call_target="tpu_custom_call" | custom-call | tf_op jit(solution)/shard_map/reduce_gram/pallas_call | solution.py:465
  72.3 0.0 copy-start
  72.3 5.6 %all-to-all-start = ((f32[32,24,1024]{2,1,0:T(8,128)}), f32[32,24,1024]{2,1,0:T(8,128)}, u32[]{:S(2)}, u32[]{:S(2)}) async-start(f32[32,24,1024]{2,1,0:T(8,128)} %get-tuple-element.15), calls=%async_computation | async-start | bytes 6291456 | tf_op jit(solution)/shard_map/all_to_all | solution.py:720
  78.0 0.0 copy-done
  78.0 30.2 %cholesky_rows.1 = f32[64,1024]{1,0:T(8,128)S(1)} custom-call(f32[2,4,4,2,72,128]{5,4,3,2,1,0:T(8,128)S(1)} %copy-done), custom_call_target="tpu_custom_call" | custom-call | flops 49999998976 | bytes 100000000 | tf_op jit(solution)/shard_map/cholesky_rows/pallas_call | solution.py:624
  108.3 0.6 collective-permute-start
  108.8 1.0 collective-permute-done
  109.8 0.7 broadcast_select_fusion
  110.5 7.3 %all-to-all-done.arrived_b = f32[32,24,1024]{2,1,0:T(8,128)} async-done(((f32[32,24,1024]{2,1,0:T(8,128)}), f32[32,24,1024]{2,1,0:T(8,128)}, u32[]{:S(2)}, u32[]{:S(2)}) %all-to-all-start) | async-done | bytes 3145760 | tf_op jit(solution)/shard_map/all_to_all | solution.py:720
  117.8 5.2 %place_slots.1 = f32[32,32,1024]{2,1,0:T(8,128)} custom-call(s32[1,512]{1,0:T(1,128)} %order_in.3, s32[1,32]{1,0:T(1,128)} %counts_in.3, f32[32,8,1024]{2,1,0:T(8,128)} %get-tuple-element.12.arrived_a, f32[32,24,1024]{2,1,0:T(8,128)} %all-to-all-done.arrived_b), custom_call_target="tpu_custom_call" | custom-call | tf_op jit(solution)/shard_map/place_slots/pallas_call | solution.py:697
  (1 shorter events, 0.0 us)
Async XLA Ops:
  72.3 5.7 %copy-start = (f32[2,4,4,2,72,128]{5,4,3,2,1,0:T(8,128)S(1)}, f32[2,4,4,2,72,128]{5,4,3,2,1,0:T(8,128)}, u32[]{:S(2)}) copy-start(f32[2,4,4,2,72,128]{5,4,3,2,1,0:T(8,128)} %get-tuple-element.16.g) | copy-start | bytes 7077892
  72.3 45.4 %all-to-all-start = ((f32[32,24,1024]{2,1,0:T(8,128)}), f32[32,24,1024]{2,1,0:T(8,128)}, u32[]{:S(2)}, u32[]{:S(2)}) async-start(f32[32,24,1024]{2,1,0:T(8,128)} %get-tuple-element.15), calls=%async_computation | async-start | bytes 6291456 | tf_op jit(solution)/shard_map/all_to_all | solution.py:720
  108.3 1.5 %collective-permute-start = (f32[32,1024]{1,0:T(8,128)S(1)}, f32[32,1024]{1,0:T(8,128)S(1)}, u32[]{:S(2)}, u32[]{:S(2)}) collective-permute-start(f32[32,1024]{1,0:T(8,128)S(1)} %slice_select_fusion), channel_id=1, source_target_pairs={{0,1},{1,0},{2,3},{3,2},{4,5},{5,4},{6,7},{7,6},{8,9},{9,8},{10,11... | collective-permute-start | bytes 393224 | tf_op jit(solution)/shard_map/ppermute | solution.py:726

commit v5 on v4

--- a/solution.py
+++ b/solution.py
@@ -573,7 +573,40 @@
     return jnp.concatenate(r_out, axis=0), jnp.concatenate(e_out, axis=0)
 
 
-def cholesky_kernel(g, out, a, r, d):
+def cholesky_kernel(g, blocks, group_rows, mean_rows, arrived, a, r, d, all_sem, stay_sem, swap_sem):
+    grp = lax.axis_index("grp")
+    dev = lax.axis_index("dev")
+    core = lax.rem(dev, 2)
+    chip = dev // 2
+    cx, cy = chip // 4, lax.rem(chip, 4)
+
+    def at_offset(dx, dy, flip):
+        return (lax.rem(cx + dx + 4, 4) * 4 + lax.rem(cy + dy + 4, 4)) * 2 + lax.rem(core + flip, 2)
+
+    def copy(src, dst, sem, at, to_dev):
+        return pltpu.make_async_remote_copy(
+            src_ref=src,
+            dst_ref=dst,
+            send_sem=sem.at[(0, *at)],
+            recv_sem=sem.at[(1, *at)],
+            device_id=(grp, to_dev),
+            device_id_type=MESH,
+        )
+
+    barrier = pltpu.get_barrier_semaphore()
+    for others in OTHERS:
+        pl.semaphore_signal(barrier, inc=1, device_id=(grp, at_offset(*others)), device_id_type=MESH)
+
+    def block_copy(i):
+        to = at_offset(*OTHERS[i])
+        return copy(blocks.at[to], arrived.at[dev], all_sem, (i,), to)
+
+    stay = pltpu.make_async_copy(blocks.at[dev], arrived.at[dev], stay_sem)
+    stay.start()
+    pl.semaphore_wait(barrier, len(OTHERS))
+    for i in range(len(OTHERS)):
+        block_copy(i).start()
+
     for i in range(NBLK):
         for j in range(i, NBLK):
             for row, size, (core_, half, x, y), start in pieces(packed(i, j)):
@@ -615,29 +648,59 @@
         return c
 
     lax.fori_loop(0, NBLK, step, 0)
-    chip = lax.axis_index("dev") // 2
-    out[...] = r[pl.ds(pl.multiple_of(chip * 64, 64), 64), :]
-
-
-def cholesky_rows(full):
+
+    half = COLS // DEVS
+    own_rows = r.at[pl.ds(pl.multiple_of(chip * 2 * half + core * half, half), half)]
+    other_rows = r.at[pl.ds(pl.multiple_of(chip * 2 * half + (1 - core) * half, half), half)]
+    partner = chip * 2 + 1 - core
+
+    @pl.when(core == 0)
+    def _():
+        copy(other_rows, group_rows, swap_sem, (0,), partner).start()
+        group_rows[...] = own_rows[...]
+        copy(other_rows, mean_rows, swap_sem, (1,), partner).wait_recv()
+        copy(other_rows, group_rows, swap_sem, (0,), partner).wait_send()
+
+    @pl.when(core == 1)
+    def _():
+        copy(other_rows, mean_rows, swap_sem, (1,), partner).start()
+        mean_rows[...] = own_rows[...]
+        copy(other_rows, group_rows, swap_sem, (0,), partner).wait_recv()
+        copy(other_rows, mean_rows, swap_sem, (1,), partner).wait_send()
+
+    for i in range(len(OTHERS)):
+        dx, dy, flip = OTHERS[i]
+        copy(blocks.at[dev], arrived.at[at_offset(-dx, -dy, flip)], all_sem, (i,), partner).wait_recv()
+        block_copy(i).wait_send()
+    stay.wait()
+
+
+def cholesky_rows(full, blocks):
     vmem = pl.BlockSpec(memory_space=pltpu.VMEM)
+    hbm = pl.BlockSpec(memory_space=pltpu.HBM)
+    dma = pltpu.SemaphoreType.DMA
+    rows = jax.ShapeDtypeStruct((COLS // DEVS, COLS), F32)
     return pl.pallas_call(
         cholesky_kernel,
-        out_shape=jax.ShapeDtypeStruct((2 * COLS // DEVS, COLS), F32),
-        in_specs=[vmem],
-        out_specs=vmem,
+        out_shape=(rows, rows, jax.ShapeDtypeStruct(blocks.shape, F32)),
+        in_specs=[vmem, hbm],
+        out_specs=(vmem, vmem, hbm),
         scratch_shapes=[
             pltpu.VMEM((COLS, COLS), F32),
             pltpu.VMEM((COLS, COLS), F32),
             pltpu.VMEM((NB, NB), F32),
+            dma((2, len(OTHERS))),
+            dma,
+            dma((2, 2)),
         ],
-        compiler_params=pltpu.CompilerParams(vmem_limit_bytes=32 << 20),
-        cost_estimate=pl.CostEstimate(flops=50_000_000_000, bytes_accessed=100_000_000, transcendentals=0),
+        compiler_params=pltpu.CompilerParams(
+            collective_id=1, has_side_effects=True, vmem_limit_bytes=62 << 20
+        ),
         name="cholesky_rows",
-    )(full)
-
-
-def place_kernel(order_in, counts_in, arrived_a, arrived_b, sketch, order, counts, stage, zero, tab_sem, in_sem, sem):
+    )(full, blocks)
+
+
+def place_kernel(order_in, counts_in, arrived_a, arrived_b, group_in, mean_in, sketch, group_out, mean_out, order, counts, stage, zero, passed, tab_sem, row_sem, in_sem, sem):
     me = lax.axis_index("dev")
     tables = [
         pltpu.make_async_copy(order_in, order, tab_sem.at[0]),
@@ -645,6 +708,10 @@
     ]
     for table in tables:
         table.start()
+    ins = [pltpu.make_async_copy(x, passed.at[i], row_sem.at[0, i]) for i, x in enumerate((group_in, mean_in))]
+    outs = [pltpu.make_async_copy(passed.at[i], x, row_sem.at[1, i]) for i, x in enumerate((group_out, mean_out))]
+    for x in ins:
+        x.start()
     zero[...] = jnp.zeros_like(zero)
     for table in tables:
         table.wait()
@@ -688,46 +755,48 @@
         return c
 
     lax.fori_loop(0, DEVS, start, 0)
+    for x, y in zip(ins, outs):
+        x.wait()
+        y.start()
     lax.fori_loop(0, DEVS, store, 0)
+    for y in outs:
+        y.wait()
     lax.fori_loop(0, DEVS, wait, 0)
 
 
-def place(block_order, counts, arrived_a, arrived_b):
+def place(block_order, counts, arrived_a, arrived_b, group_rows, mean_rows):
     hbm = pl.BlockSpec(memory_space=pltpu.HBM)
     return pl.pallas_call(
         place_kernel,
-        out_shape=jax.ShapeDtypeStruct((DEVS, KEEP, COLS), F32),
-        in_specs=[hbm] * 4,
-        out_specs=hbm,
+        out_shape=(
+            jax.ShapeDtypeStruct((DEVS, KEEP, COLS), F32),
+            jax.ShapeDtypeStruct(group_rows.shape, F32),
+            jax.ShapeDtypeStruct(mean_rows.shape, F32),
+        ),
+        in_specs=[hbm] * 6,
+        out_specs=(hbm, hbm, hbm),
         scratch_shapes=[
             pltpu.SMEM((1, POSITIONS), I32),
             pltpu.SMEM((1, DEVS), I32),
             pltpu.VMEM((DEVS, KEEP, COLS), F32),
             pltpu.VMEM((KEEP, COLS), F32),
+            pltpu.VMEM((2, COLS // DEVS, COLS), F32),
             pltpu.SemaphoreType.DMA((2,)),
+            pltpu.SemaphoreType.DMA((2, 2)),
             pltpu.SemaphoreType.DMA((DEVS, 2)),
             pltpu.SemaphoreType.DMA((DEVS,)),
         ],
         compiler_params=pltpu.CompilerParams(vmem_limit_bytes=62 << 20),
         name="place_slots",
-    )(block_order, counts, arrived_a, arrived_b)
+    )(block_order, counts, arrived_a, arrived_b, group_rows, mean_rows)
 
 
 def body(matrix, block_order, counts, sign_bits, row_mask):
     early, late, kept = mix(matrix, block_order, counts, sign_bits, row_mask)
     full, early = reduce_gram(kept, early)
-    late, full = lax.optimization_barrier((late, full))
-    late = lax.all_to_all(late, "dev", split_axis=0, concat_axis=0, tiled=True)
-    rows = cholesky_rows(full)
-    half = rows.shape[0] // 2
-    first = lax.rem(lax.axis_index("dev"), 2) == 0
-    mine = jnp.where(first, rows[:half], rows[half:])
-    other = jnp.where(first, rows[half:], rows[:half])
-    other = lax.ppermute(other, "dev", [(d, d ^ 1) for d in range(DEVS)])
-    sketch = place(block_order, counts, early, late)
-    group_factor = jnp.where(first, mine, other)[None]
-    factor = jnp.where(first, other, mine)
-    return sketch.reshape(DEVS * KEEP, COLS), group_factor, factor
+    group_rows, mean_rows, late = cholesky_rows(full, late)
+    sketch, group_rows, mean_rows = place(block_order, counts, early, late, group_rows, mean_rows)
+    return sketch.reshape(DEVS * KEEP, COLS), group_rows[None], mean_rows
 
 
 def solution(mesh):

time: 123 us -> 125 us (1.016)
  Pallas kernels: 107 us -> 124 us
  waiting for transfers between devices: 8.25 us -> 0 us
  starting transfers between devices: 6.18 us -> 0 us
    pallas_call x2, Pallas kernels: 35.4 us -> 51.8 us  [the longest x1 46.3 us: cholesky_rows(): pl.pallas_call(cholesky_kernel, out_shape=(rows, rows, jax.ShapeDtypeStru...]
    all_to_all x1 -> x0, waiting for transfers between devices: 7.26 us -> none  [body(): late = lax.all_to_all(late, 'dev', split_axis=0, concat_axis=0, tiled=True)]
    all_to_all x1 -> x0, starting transfers between devices: 5.63 us -> none  [body(): late = lax.all_to_all(late, 'dev', split_axis=0, concat_axis=0, tiled=True)]
  transfers between devices with their start and end apart: 2 -> 0, of which waited for: 2 -> 0; matrix products, arithmetic and copies ran while one was open for 1% -> 0% of each run, Pallas kernels for 25% -> 0%
where the time goes in v5:
time: 125 us; the launch traced here: 124 us
  Pallas kernels  124 us (99%)
    pallas_call x1, Pallas kernels, reduce_gram(): pl.pallas_call(reduce_kernel, out_shape=(jax.ShapeDtypeStruct((2, 4, 4, 2...  62.8 us
    pallas_call x1, Pallas kernels, cholesky_rows(): pl.pallas_call(cholesky_kernel, out_shape=(rows, rows, jax.ShapeDtypeStru...  46.3 us
    pallas_call x1, Pallas kernels, mix(): pl.pallas_call(mix_kernel, out_shape=(jax.ShapeDtypeStruct((DEVS, EARLY,...  8.84 us
    pallas_call x1, Pallas kernels, place(): pl.pallas_call(place_kernel, out_shape=(jax.ShapeDtypeStruct((DEVS, KEEP,...  5.55 us

profile of v5, /device:TPU:1, one launch (start us, length us, event | category | flops | bytes accessed | tf_op | source)
XLA Modules:
  0.0 124.3 jit_solution(924127692682865268)
XLA Ops:
  0.6 8.8 %mix_rows.1 = (f32[32,8,1024]{2,1,0:T(8,128)}, f32[32,24,1024]{2,1,0:T(8,128)}, f32[512,1024]{1,0:T(8,128)}) custom-call(s32[1,512]{1,0:T(1,128)} %order_in.3, s32[1,32]{1,0:T(1,128)} %counts_in.3, f32[2048,1024]{1,0:T(8,128)} %matrix.1, s32[1,512,128]{2,1,0:T(8,128)} %sign_bits.1, s32[1,512,128]{2,1,0:T(8,128)} %row_mask.1), custom_call_target="tpu_custom_call" | custom-call | tf_op jit(solution)/shard_map/mix_rows/pallas_call | solution.py:138
  9.5 62.8 %reduce_gram.1 = (f32[2,4,4,2,72,128]{5,4,3,2,1,0:T(8,128)}, f32[32,8,1024]{2,1,0:T(8,128)}) custom-call(f32[512,1024]{1,0:T(8,128)} %get-tuple-element.14.kept, f32[32,8,1024]{2,1,0:T(8,128)} %get-tuple-element.15.blocks), custom_call_target="tpu_custom_call" | custom-call | tf_op jit(solution)/shard_map/reduce_gram/pallas_call | solution.py:465
  72.3 46.3 %cholesky_rows.1 = (f32[32,1024]{1,0:T(8,128)}, f32[32,1024]{1,0:T(8,128)}, f32[32,24,1024]{2,1,0:T(8,128)}) custom-call(f32[2,4,4,2,72,128]{5,4,3,2,1,0:T(8,128)} %get-tuple-element.17.g, f32[32,24,1024]{2,1,0:T(8,128)} %get-tuple-element.18.blocks), custom_call_target="tpu_custom_call" | custom-call | tf_op jit(solution)/shard_map/cholesky_rows/pallas_call | solution.py:683
  118.6 5.6 %place_slots.1 = (f32[32,32,1024]{2,1,0:T(8,128)}, f32[32,1024]{1,0:T(8,128)}, f32[32,1024]{1,0:T(8,128)}) custom-call(s32[1,512]{1,0:T(1,128)} %order_in.3, s32[1,32]{1,0:T(1,128)} %counts_in.3, f32[32,8,1024]{2,1,0:T(8,128)} %get-tuple-element.16.arrived_a, f32[32,24,1024]{2,1,0:T(8,128)} %get-tuple-element.19.arrived_b, ...), custom_call_target="tpu_custom_call" | custom-call | tf_op jit(solution)/shard_map/place_slots/pallas_call | solution.py:769
